TPU v7x, 32 devices: a whole 2x2x4 slice. The times are simulated.
32 devices in a mesh: groups: 2 (over y), seq: 4 (over z), heads: 2 (over x), sub: 2 (over core).
Axes of the slice: x: 2, y: 2, z: 4, core: 2. Of those that a mesh axis runs over, the one named last changes fastest.
Arguments:
- queries: bfloat16 [4096, 2048], P(('groups', 'seq', 'heads', 'sub')), parts along dimension 0, may hold values from -12.5 to 12.5
- new_keys: bfloat16 [4096, 2048], P(('groups', 'seq', 'heads', 'sub')), parts along dimension 0, may hold values from -5 to 5
- new_values: bfloat16 [4096, 2048], P(('groups', 'seq', 'heads', 'sub')), parts along dimension 0, may hold values from -5 to 5
- cache_keys: bfloat16 [8192, 2048], P(('groups', 'seq'), ('heads', 'sub')), parts along dimension 0, may hold values from -5 to 5
- cache_values: bfloat16 [8192, 2048], P(('groups', 'seq'), ('heads', 'sub')), parts along dimension 0, may hold values from -5 to 5
- selection: int32 [8, 16, 8], P(('groups', 'seq'), ('heads', 'sub')), parts along dimension 0, may hold values from 0 to 7, as said below
Outputs:
- attended: bfloat16 [4096, 2048], P(('groups', 'seq', 'heads', 'sub')), parts along dimension 0
There are 2 independent parts, one for each index of `groups`. A program takes and returns all parts, laid end to end along the dimension named above; each array names one. Nothing has to cross between parts.
Inputs may be any that keep to these rules, and one draw needn't show every extreme that they name: `selection`: every selected block precedes the span; the 8 blocks of one query block and head are different. For one index of seq and one index of heads+sub, of the 32 selections of that device's query blocks and heads (heads taken in order from index times 4), exactly 8 names a block held by each index of seq (blocks index * 2 to index * 2 + 1).
All inputs are finite; a program needn't handle non-finite values.
Results may differ from a plain program's by a relative error of at most 0.0023.
Values may be sent and summed in bfloat16 or wider, within the bound.
No kernel may reach another device: no remote copies, remote signals or barrier semaphores. Data moves between devices by JAX's collectives and lax.ppermute only.
A program may use at most 128 MiB of HBM per device.

v0:
```python
import functools
import math

import jax
import jax.numpy as jnp
from jax import lax
from jax.experimental import pallas as pl
from jax.experimental.pallas import tpu as pltpu
from jax.sharding import PartitionSpec as P

HD = 128
BLOCK = 512


def order_ranks(owners):
    length = owners.shape[-1]
    counter = jnp.arange(length)
    earlier = counter[None, :] < counter[:, None]
    same_owner = owners[..., :, None] == owners[..., None, :]
    return jnp.sum(jnp.logical_and(same_owner, earlier), axis=-1)


def one_hot(values, length):
    return (values[..., None] == jnp.arange(length)).astype(jnp.float32)


def own_partial(query_blocks, key_blocks, value_blocks, scaling):
    scores = (
        jnp.einsum("bqhd,bkhd->bhqk", query_blocks, key_blocks, preferred_element_type=jnp.float32)
        * scaling
    )
    length = query_blocks.shape[1]
    causal = jnp.arange(length)[:, None] >= jnp.arange(length)[None, :]
    scores = jnp.where(causal, scores, -jnp.inf)
    highest = jnp.max(scores, axis=-1)
    weights = jnp.exp(scores - highest[..., None])
    totals = jnp.sum(weights, axis=-1)
    mixed = jnp.einsum(
        "bhqk,bkhd->bhqd",
        weights.astype(jnp.bfloat16),
        value_blocks,
        preferred_element_type=jnp.float32,
    )
    return (mixed, highest, totals)


def tile_partial(query_blocks, tile_pair, scaling):
    head_size = query_blocks.shape[-1]
    scores = (
        jnp.einsum(
            "bqhd,bhkd->bhqk",
            query_blocks,
            tile_pair[..., :head_size],
            preferred_element_type=jnp.float32,
        )
        * scaling
    )
    highest = jnp.max(scores, axis=-1)
    weights = jnp.exp(scores - highest[..., None])
    totals = jnp.sum(weights, axis=-1)
    mixed = jnp.einsum(
        "bhqk,bhkd->bhqd",
        weights.astype(jnp.bfloat16),
        tile_pair[..., head_size:],
        preferred_element_type=jnp.float32,
    )
    return (mixed, highest, totals)


def merge_parts(parts):
    top = parts[0][1]
    for part in parts[1:]:
        top = jnp.maximum(top, part[1])
    numer = jnp.zeros(parts[0][0].shape, jnp.float32)
    denom = jnp.zeros(parts[0][2].shape, jnp.float32)
    for part in parts:
        factor = jnp.exp(part[1] - top)
        numer = numer + factor[..., None] * part[0]
        denom = denom + factor * part[2]
    return numer / denom[..., None]


def sparse_body(queries, new_keys, new_values, cache_keys, cache_values, selection):
    heads_q, heads_k, heads_v = (
        lax.all_to_all(queries, ("heads", "sub"), split_axis=1, concat_axis=0, tiled=True),
        lax.all_to_all(new_keys, ("heads", "sub"), split_axis=1, concat_axis=0, tiled=True),
        lax.all_to_all(new_values, ("heads", "sub"), split_axis=1, concat_axis=0, tiled=True),
    )
    qblocks, head_count, top_count = selection.shape
    head_size = HD
    scaling = head_size ** (-0.5)
    shaped = (qblocks, BLOCK, head_count, head_size)
    query_blocks = heads_q.reshape(shaped)
    own = own_partial(query_blocks, heads_k.reshape(shaped), heads_v.reshape(shaped), scaling)
    seq_count = lax.axis_size("seq")
    myself = lax.axis_index("seq")
    cache_blocks = cache_keys.shape[0] // BLOCK
    tile_count = cache_blocks * head_count
    request_count = qblocks * head_count * top_count
    capacity = -(-request_count // seq_count)
    requests_all = lax.all_gather(selection, "seq", axis=0, tiled=True).reshape(
        seq_count, request_count
    )
    head_of = jnp.arange(request_count) // top_count % head_count
    my_requests = selection.reshape(request_count)
    my_owner = my_requests // cache_blocks
    my_slot = my_owner * capacity + order_ranks(my_owner)
    key_tiles = cache_keys.reshape(cache_blocks, BLOCK, head_count, head_size).transpose(0, 2, 1, 3)
    value_tiles = cache_values.reshape(cache_blocks, BLOCK, head_count, head_size).transpose(
        0, 2, 1, 3
    )
    tile_set = jnp.concatenate([key_tiles, value_tiles], axis=-1).reshape(
        tile_count, BLOCK, 2 * head_size
    )
    their_owner = requests_all // cache_blocks
    local_tile = requests_all % cache_blocks * head_count + head_of[None, :]
    served = (their_owner == myself).astype(jnp.float32)
    slot_pick = one_hot(order_ranks(their_owner), capacity) * served[..., None]
    picking = jnp.einsum("erc,erl->ecl", slot_pick, one_hot(local_tile, tile_count)).astype(
        jnp.bfloat16
    )
    parts = [own]
    outgoing = jnp.einsum(
        "ecl,lkf->eckf", picking, tile_set, preferred_element_type=jnp.float32
    ).astype(jnp.bfloat16)
    incoming = lax.all_to_all(outgoing, "seq", split_axis=0, concat_axis=0, tiled=True)
    fetched = incoming.reshape(seq_count * capacity, BLOCK, 2 * head_size)[my_slot]
    fetched = fetched.reshape(qblocks, head_count, top_count, BLOCK, 2 * head_size)
    for turn in range(top_count):
        parts.append(tile_partial(query_blocks, fetched[:, :, turn], scaling))
    result = merge_parts(parts)
    result = (
        result.transpose(0, 2, 1, 3)
        .reshape(qblocks * BLOCK, head_count * head_size)
        .astype(jnp.bfloat16)
    )
    return lax.all_to_all(result, ("heads", "sub"), split_axis=0, concat_axis=1, tiled=True)


STAT = 16
UNIT = 32767.0
LEAST = 1.2e-34
C2 = math.log2(math.e) * HD**-0.5


def scores_of(q, k, mask=None):
    s = lax.dot_general(k, q, (((1,), (1,)), ((), ())), preferred_element_type=jnp.float32)
    return s if mask is None else jnp.where(mask, s, -jnp.inf)


def weights_of(s):
    m = jnp.max(s, axis=0, keepdims=True)
    p = jnp.exp2((s - m) * C2)
    return p.astype(jnp.bfloat16), m * C2, jnp.sum(p, axis=0, keepdims=True)


def values_of(v, w, v_dim):
    return lax.dot_general(v, w, (((v_dim,), (0,)), ((), ())), preferred_element_type=jnp.float32)


def attend(tiles):
    count = len(tiles)
    s, w, parts = {}, {}, []
    for t in range(count + 2):
        if t < count:
            s[t] = tiles[t][0]()
        if 1 <= t <= count:
            w[t - 1] = weights_of(s.pop(t - 1))
        if t >= 2:
            weights, m, total = w.pop(t - 2)
            parts.append((tiles[t - 2][1](weights), m, total))
    return parts


def join(parts):
    top = functools.reduce(jnp.maximum, [m for _, m, _ in parts])
    factors = [jnp.exp2(m - top) for _, m, _ in parts]
    numer = sum(f * o for f, (o, _, _) in zip(factors, parts))
    denom = sum(f * t for f, (_, _, t) in zip(factors, parts))
    return numer, top, denom


def put(out_ref, heads):
    width, rows = len(heads) * HD, heads[0][0].shape[1]
    at = lax.broadcasted_iota(jnp.int32, (STAT, rows), 0)
    stats = jnp.zeros((STAT, rows), jnp.float32)
    for h, (numer, top, denom) in enumerate(heads):
        most = jnp.maximum(jnp.max(jnp.abs(numer), axis=0, keepdims=True), LEAST)
        code = jnp.round(numer * (UNIT / most))
        out_ref[h * HD : (h + 1) * HD, :] = code.astype(jnp.int32).astype(jnp.int16)
        for j, value in enumerate((top + jnp.log2(denom), jnp.log2(most / (UNIT * denom)))):
            whole = jnp.floor(value)
            stats = jnp.where(at == 4 * h + 2 * j, whole, stats)
            stats = jnp.where(at == 4 * h + 2 * j + 1, jnp.round((value - whole) * UNIT), stats)
    out_ref[width : width + STAT, :] = stats.astype(jnp.int32).astype(jnp.int16)


def take(ref):
    width = ref.shape[0] - STAT
    stats = ref[width : width + STAT, :].astype(jnp.int32).astype(jnp.float32)
    heads = []
    for h in range(width // HD):
        code = ref[h * HD : (h + 1) * HD, :].astype(jnp.int32).astype(jnp.float32)
        weight = stats[4 * h : 4 * h + 1] + stats[4 * h + 1 : 4 * h + 2] * (1.0 / UNIT)
        unit = stats[4 * h + 2 : 4 * h + 3] + stats[4 * h + 3 : 4 * h + 4] * (1.0 / UNIT)
        heads.append((code, weight, unit))
    return heads


def join_taken(taken):
    top = functools.reduce(jnp.maximum, [w for _, w, _ in taken])
    numer = sum(code * jnp.exp2(w - top + unit) for code, w, unit in taken)
    denom = sum(jnp.exp2(w - top) for _, w, _ in taken)
    return numer, top, denom


def cached_tiles(q_of, ck_ref, cvt_ref, h):
    cols = slice(h * HD, (h + 1) * HD)
    tiles = []
    for b in range(ck_ref.shape[0] // BLOCK):
        rows = slice(b * BLOCK, (b + 1) * BLOCK)
        tiles.append(
            (
                lambda rows=rows: scores_of(q_of(cols), ck_ref[rows, cols]),
                lambda w, rows=rows: values_of(cvt_ref[cols, rows], w, 1),
            )
        )
    return tiles


def attend_heads(tiles_of_heads):
    parts = attend([t for tiles in tiles_of_heads for t in tiles])
    heads = []
    for tiles in tiles_of_heads:
        heads.append(join(parts[: len(tiles)]))
        parts = parts[len(tiles) :]
    return heads


def cached_kernel(q_ref, ck_ref, cvt_ref, out_ref):
    heads = range(ck_ref.shape[1] // HD)
    q_of = lambda cols: q_ref[:, cols]
    put(out_ref, attend_heads([cached_tiles(q_of, ck_ref, cvt_ref, h) for h in heads]))


def own_kernel(mine, order_ref, *refs):
    q_ref, *kv_refs, ck_ref, cvt_ref, out_ref = refs
    width = ck_ref.shape[1]
    rows = q_ref.shape[0]
    step = kv_refs[0].shape[0]

    def positions(shape, axis, pieces):
        at = lax.broadcasted_iota(jnp.int32, shape, axis)
        place = jnp.zeros(shape, jnp.int32)
        for i, d in enumerate(pieces):
            place = jnp.where(at // step == i, order_ref[d] * step + at % step, place)
        return place

    shape = (step * len(kv_refs), rows)
    mask = positions(shape, 1, mine) >= positions(shape, 0, range(len(kv_refs)))
    q_of = lambda cols: q_ref[:, cols]
    heads = []
    for h in range(width // HD):
        cols = slice(h * HD, (h + 1) * HD)
        vcols = slice(width + h * HD, width + (h + 1) * HD)
        own = (
            lambda cols=cols: scores_of(
                q_ref[:, cols], jnp.concatenate([r[:, cols] for r in kv_refs], axis=0), mask
            ),
            lambda w, vcols=vcols: values_of(
                jnp.concatenate([r[:, vcols] for r in kv_refs], axis=0), w, 0
            ),
        )
        heads.append([own] + cached_tiles(q_of, ck_ref, cvt_ref, h))
    put(out_ref, attend_heads(heads))


def merge_kernel(*refs):
    *in_refs, out_ref = refs
    put(out_ref, [join_taken(taken) for taken in zip(*[take(r) for r in in_refs])])


def final_kernel(count, *refs):
    in_refs, out_refs = refs[:count], refs[count:]
    step = out_refs[0].shape[0]
    for h, taken in enumerate(zip(*[take(r) for r in in_refs])):
        numer, _, denom = join_taken(taken)
        value = jnp.transpose(numer * (1.0 / denom)).astype(jnp.bfloat16)
        for i, out_ref in enumerate(out_refs):
            out_ref[:, h * HD : (h + 1) * HD] = value[i * step : (i + 1) * step]


def pick_kernel(pieces, count, order_ref, *refs):
    in_refs, out_refs, done = refs[:count], refs[count:-1], refs[-1]
    width = out_refs[0].shape[1] // count
    copies = []
    for d, out_ref in zip(pieces, out_refs):
        start = pl.multiple_of(order_ref[d] * width, width)
        for i, ref in enumerate(in_refs):
            source, target = ref.at[:, pl.ds(start, width)], out_ref.at[:, i * width : (i + 1) * width]
            copies.append(pltpu.make_async_copy(source, target, done.at[len(copies)]))
            copies[-1].start()
    for copy in copies:
        copy.wait()


def slice_kernel(pieces, order_ref, ref, *out_refs):
    width = out_refs[0].shape[1]
    for d, out_ref in zip(pieces, out_refs):
        out_ref[...] = ref[:, pl.ds(pl.multiple_of(order_ref[d] * width, width), width)]


def stack_kernel(count, *refs):
    out_ref = refs[-1]
    step = refs[0].shape[0]
    for i in range(count):
        out_ref[i * step : (i + 1) * step, :] = refs[i][...]


def place_kernel(order_ref, *refs):
    *pieces, out_ref = refs
    width = pieces[0].shape[1]
    for d, piece in enumerate(pieces):
        start = pl.multiple_of(order_ref[d] * width, width)
        out_ref[:, pl.ds(start, width)] = piece[...]


def move(kernel, copies, scalars, arrays, outs, unread=()):
    read = 1 + len(arrays)

    def without_unread(*refs):
        kernel(*refs[:read], *refs[read + len(unread) :])

    return pl.pallas_call(
        without_unread,
        out_shape=outs,
        in_specs=[pl.BlockSpec(memory_space=pltpu.SMEM)]
        + [pl.BlockSpec(memory_space=pl.ANY)] * (len(arrays) + len(unread)),
        out_specs=[pl.BlockSpec(memory_space=pltpu.VMEM)] * len(outs),
        scratch_shapes=[pltpu.SemaphoreType.DMA((copies,))],
        cost_estimate=pl.CostEstimate(flops=0, bytes_accessed=2 * 4 * outs[0].size, transcendentals=0),
    )(scalars, *arrays, *unread)


def call(kernel, arrays, outs, flops=0, exps=0, scalars=None, unread=()):
    moved = sum(a.size * a.dtype.itemsize for a in arrays)
    moved += sum(math.prod(o.shape) * o.dtype.itemsize for o in outs)
    first = [] if scalars is None else [scalars]
    return pl.pallas_call(
        kernel,
        out_shape=outs,
        in_specs=[pl.BlockSpec(memory_space=pltpu.SMEM)] * len(first)
        + [pl.BlockSpec(memory_space=pltpu.VMEM)] * len(arrays)
        + [pl.BlockSpec(memory_space=pl.ANY)] * len(unread),
        out_specs=[pl.BlockSpec(memory_space=pltpu.VMEM)] * len(outs),
        compiler_params=pltpu.CompilerParams(vmem_limit_bytes=16 * 1024 * 1024),
        cost_estimate=pl.CostEstimate(flops=flops, bytes_accessed=moved, transcendentals=exps),
    )(*first, *arrays, *unread)


def dense_body(queries, new_keys, new_values, cache_keys, cache_values):
    seq_count = lax.axis_size("seq")
    shares = lax.axis_size("heads") * lax.axis_size("sub")
    me = lax.axis_index("heads") * lax.axis_size("sub") + lax.axis_index("sub")
    step, width = queries.shape[0], queries.shape[1] // shares
    cached = cache_keys.shape[0]
    each = shares // CHUNKS
    rows = each * step
    chunk = jax.ShapeDtypeStruct((rows, width), jnp.bfloat16)
    piece = jax.ShapeDtypeStruct((step, width), jnp.bfloat16)
    pair = jax.ShapeDtypeStruct((step, 2 * width), jnp.bfloat16)
    packed = jax.ShapeDtypeStruct((width + STAT, rows), jnp.int16)
    tile_flops = 4 * rows * cached * width
    tile_exps = rows * cached * (width // HD)

    def swap(x, d):
        return lax.ppermute(x, ("heads", "sub"), [(i, i ^ d) for i in range(shares)])

    def along(x, bit):
        return lax.ppermute(x, "seq", [(i, i ^ bit) for i in range(seq_count)])

    def after(x, unread):
        like = jax.ShapeDtypeStruct(x.shape, x.dtype)
        return call(functools.partial(stack_kernel, 1), [x], [like], unread=unread)[0] if unread else x

    order = jnp.stack([me ^ d for d in range(shares)]).astype(jnp.int32)
    cache_vt = cache_values.T
    context = [cache_keys, cache_vt]

    def attend(q):
        return call(cached_kernel, [q, *context], [packed], tile_flops, tile_exps)[0]

    def attend_own(q, pieces):
        return call(
            functools.partial(own_kernel, pieces),
            [q, *kv, *context],
            [packed],
            tile_flops * 3 // 2,
            tile_exps * 3 // 2,
            order,
        )[0]

    def merge(mine, got):
        return call(merge_kernel, [mine, got], [packed])[0]

    def end(parts, pieces):
        ended = call(functools.partial(final_kernel, len(parts)), parts, [piece] * each)
        return [swap(x, d) if d else x for x, d in zip(ended, pieces)]

    pieces_a, pieces_b = range(each), range(each, shares)

    def pick(arrays, pieces, out, unread=()):
        kernel = functools.partial(pick_kernel, pieces, len(arrays))
        count = len(pieces)
        return move(kernel, count * len(arrays), order, arrays, [out] * count, unread)

    def slices(pieces):
        kernel = functools.partial(slice_kernel, pieces)
        return call(kernel, [queries], [piece] * each, scalars=order)

    q = [swap(x, d) if d else x for x, d in zip(slices(pieces_a), pieces_a)]
    a = call(functools.partial(stack_kernel, each), q, [chunk])[0]
    q = slices(pieces_b)
    a2, a1 = along(a, 2), along(a, 1)
    q = [swap(x, d) for x, d in zip(q, pieces_b)]
    b = call(functools.partial(stack_kernel, each), q, [chunk])[0]
    b2, b1 = along(b, 2), along(b, 1)
    kv = pick([new_keys, new_values], range(shares), pair, [b, cache_vt])
    kv = [swap(x, d) if d else x for d, x in enumerate(kv)]
    part_a2, part_a1 = attend(a2), attend(a1)
    b3 = along(after(b2, [part_a2, part_a1]), 1)
    part_b2 = attend(b2)
    a3 = along(after(a2, [part_b2, b1, *kv[1:]]), 1)
    got_b2 = along(attend(b3), 1)
    got_a2 = along(attend(a3), 1)
    part_b2 = merge(part_b2, got_b2)
    from_b2 = along(part_b2, 2)
    from_b1 = along(after(attend(b1), [part_b2]), 1)
    part_a2 = merge(part_a2, got_a2)
    from_a2 = along(part_a2, 2)
    from_a1 = along(after(part_a1, [part_a2]), 1)
    out_b = end([attend_own(b, pieces_b), from_b2, from_b1], pieces_b)
    out_a = end([attend_own(a, pieces_a), from_a2, from_a1], pieces_a)
    results = [*out_a, *out_b]
    out = jax.ShapeDtypeStruct((step, shares * width), jnp.bfloat16)
    return call(place_kernel, results, [out], scalars=order)[0]


CHUNKS = 2


def power_of_two(n):
    return n & (n - 1) == 0


def body(queries, new_keys, new_values, cache_keys, cache_values, selection):
    qblocks, head_count, top_count = selection.shape
    seq_count = lax.axis_size("seq")
    shares = lax.axis_size("heads") * lax.axis_size("sub")
    every = top_count == cache_keys.shape[0] // BLOCK * seq_count and qblocks == 1
    fits = seq_count == 4 and power_of_two(shares) and shares % CHUNKS == 0
    if every and fits and 4 * head_count <= STAT:
        return dense_body(queries, new_keys, new_values, cache_keys, cache_values)
    return sparse_body(queries, new_keys, new_values, cache_keys, cache_values, selection)


def solution(mesh):
    in_specs = (
        P(("groups", "seq", "heads", "sub"), None),
        P(("groups", "seq", "heads", "sub"), None),
        P(("groups", "seq", "heads", "sub"), None),
        P(("groups", "seq"), ("heads", "sub")),
        P(("groups", "seq"), ("heads", "sub")),
        P(("groups", "seq"), ("heads", "sub"), None),
    )
    out_specs = P(("groups", "seq", "heads", "sub"), None)
    return jax.shard_map(body, mesh=mesh, in_specs=in_specs, out_specs=out_specs, check_vma=False)
```

profile of v0, /device:TPU:0, one launch (start us, length us, event | category | flops | bytes accessed | tf_op | source)
XLA Modules:
  0.0 84.5 jit_solution(2184567600512604446)
XLA Ops:
  0.0 0.1 pad_add_fusion.order_ref.refs_0_
  0.1 1.0 %copy-done.4 = bf16[128,2048]{1,0:T(8,128)(2,1)S(1)} copy-done((bf16[128,2048]{1,0:T(8,128)(2,1)S(1)}, bf16[128,2048]{1,0:T(8,128)(2,1)}, u32[]{:S(2)}) %copy-start.4) | copy-done | bytes 524312
  1.1 0.6 shard_map.55
  1.7 0.5 collective-permute-start
  2.2 1.0 %collective-permute-done.refs_1_ = bf16[128,512]{1,0:T(8,128)(2,1)S(1)} collective-permute-done((bf16[128,512]{1,0:T(8,128)(2,1)S(1)}, bf16[128,512]{1,0:T(8,128)(2,1)S(1)}, u32[]{:S(2)}, u32[]{:S(2)}) %collective-permute-start) | collective-permute-done | bytes 131104 | tf_op jit(solution)/shard_map/ppermute | solution.py:377
  3.2 3.0 %collective-permute-start.12 = (bf16[256,512]{1,0:T(8,128)(2,1)S(1)}, bf16[256,512]{1,0:T(8,128)(2,1)}, u32[]{:S(2)}, u32[]{:S(2)}) collective-permute-start(bf16[256,512]{1,0:T(8,128)(2,1)S(1)} %shard_map.56.refs_0_), channel_id=1, source_target_pairs={{0,4},{4,0},{8,12},{12,8},{1,5},{5,1},{9,13},{13,9},{2,6},{6,2},{1... | collective-permute-start | bytes 786440 | tf_op jit(solution)/shard_map/ppermute | solution.py:380
  6.2 2.6 %collective-permute-start.6 = (bf16[256,512]{1,0:T(8,128)(2,1)S(1)}, bf16[256,512]{1,0:T(8,128)(2,1)S(1)}, u32[]{:S(2)}, u32[]{:S(2)}) collective-permute-start(bf16[256,512]{1,0:T(8,128)(2,1)S(1)} %shard_map.56.refs_0_), channel_id=1, source_target_pairs={{0,8},{4,12},{8,0},{12,4},{1,9},{5,13},{9,1},{13,5},{2,10},{6,14},... | collective-permute-start | bytes 786440 | tf_op jit(solution)/shard_map/ppermute | solution.py:380
  8.8 0.6 shard_map.57
  9.4 1.6 %collective-permute-start.1 = (bf16[128,512]{1,0:T(8,128)(2,1)S(1)}, bf16[128,512]{1,0:T(8,128)(2,1)S(1)}, u32[]{:S(2)}, u32[]{:S(2)}) collective-permute-start(bf16[128,512]{1,0:T(8,128)(2,1)S(1)} %get-tuple-element.19), channel_id=1, source_target_pairs={{0,2},{1,3},{2,0},{3,1},{4,6},{5,7},{6,4},{7,5},{8,10},{9,11},{10,... | collective-permute-start | bytes 393224 | tf_op jit(solution)/shard_map/ppermute | solution.py:377
  10.9 0.0 collective-permute-start.2
  10.9 4.0 %collective-permute-done.1.refs_0_ = bf16[128,512]{1,0:T(8,128)(2,1)S(1)} collective-permute-done((bf16[128,512]{1,0:T(8,128)(2,1)S(1)}, bf16[128,512]{1,0:T(8,128)(2,1)S(1)}, u32[]{:S(2)}, u32[]{:S(2)}) %collective-permute-start.1) | collective-permute-done | bytes 131104 | tf_op jit(solution)/shard_map/ppermute | solution.py:377
  15.0 1.8 %collective-permute-done.2.refs_1_ = bf16[128,512]{1,0:T(8,128)(2,1)S(1)} collective-permute-done((bf16[128,512]{1,0:T(8,128)(2,1)S(1)}, bf16[128,512]{1,0:T(8,128)(2,1)S(1)}, u32[]{:S(2)}, u32[]{:S(2)}) %collective-permute-start.2) | collective-permute-done | bytes 131104 | tf_op jit(solution)/shard_map/ppermute | solution.py:377
  16.7 0.0 copy-start.2
  16.8 0.4 collective-permute-start.7
  17.2 0.0 copy-done.9
  17.2 1.3 %copy.6 = bf16[1024,512]{0,1:T(8,128)(2,1)} copy(bf16[1024,512]{1,0:T(8,128)(2,1)S(1)} %copy-done.9) | data formatting | bytes 2097152 | tf_op args[4]
  18.5 0.5 collective-permute-start.8
  19.0 3.1 %shard_map.59 = (bf16[128,1024]{1,0:T(8,128)(2,1)}, bf16[128,1024]{1,0:T(8,128)(2,1)}, bf16[128,1024]{1,0:T(8,128)(2,1)}, bf16[128,1024]{1,0:T(8,128)(2,1)}) custom-call(s32[4]{0:T(128)} %copy-done.7, bf16[128,2048]{1,0:T(8,128)(2,1)} %refs_1_.1, bf16[128,2048]{1,0:T(8,128)(2,1)} %refs_2_.1, bf16[256,512]{1,0:T(8,128)(2,1)} %copy-done.2, ...), custom_call_target="tpu_custom_call" | custom-call | bytes 1048576 | tf_op jit(solution)/shard_map/pallas_call | solution.py:334
  22.2 0.1 collective-permute-start.3
  22.3 0.0 collective-permute-done.12.q_ref
  22.3 1.5 %collective-permute-start.4 = (bf16[128,1024]{1,0:T(8,128)(2,1)}, bf16[128,1024]{1,0:T(8,128)(2,1)S(1)}, u32[]{:S(2)}, u32[]{:S(2)}) collective-permute-start(bf16[128,1024]{1,0:T(8,128)(2,1)} %get-tuple-element.23), channel_id=1, source_target_pairs={{0,2},{1,3},{2,0},{3,1},{4,6},{5,7},{6,4},{7,5},{8,10},{9,11},{10,... | collective-permute-start | bytes 786440 | tf_op jit(solution)/shard_map/ppermute | solution.py:377
  23.8 2.3 %collective-permute-done.6.q_ref.refs_0_ = bf16[256,512]{1,0:T(8,128)(2,1)S(1)} collective-permute-done((bf16[256,512]{1,0:T(8,128)(2,1)S(1)}, bf16[256,512]{1,0:T(8,128)(2,1)S(1)}, u32[]{:S(2)}, u32[]{:S(2)}) %collective-permute-start.6) | collective-permute-done | bytes 262176 | tf_op jit(solution)/shard_map/ppermute | solution.py:380
  26.2 0.0 collective-permute-start.5
  26.2 2.8 %shard_map.66.refs_0_.refs_2_ = s16[528,256]{1,0:T(8,128)(2,1)S(1)} custom-call(bf16[256,512]{1,0:T(8,128)(2,1)} %collective-permute-done.12.q_ref, bf16[1024,512]{1,0:T(8,128)(2,1)S(1)} %copy-done.1, bf16[512,1024]{1,0:T(8,128)(2,1)S(1)} %bitcast.6), custom_call_target="tpu_custom_call" | custom-call | flops 536870912 | bytes 2629632 | tf_op jit(solution)/shard_map/pallas_call | solution.py:349
  28.9 1.8 %shard_map.61.refs_0_.refs_1_ = s16[528,256]{1,0:T(8,128)(2,1)S(1)} custom-call(bf16[256,512]{1,0:T(8,128)(2,1)S(1)} %collective-permute-done.6.q_ref.refs_0_, bf16[1024,512]{1,0:T(8,128)(2,1)S(1)} %copy-done.1, bf16[512,1024]{1,0:T(8,128)(2,1)S(1)} %bitcast.7), custom_call_target="tpu_custom_call" | custom-call | flops 536870912 | bytes 2629632 | tf_op jit(solution)/shard_map/pallas_call | solution.py:349
  30.8 1.4 %collective-permute-done.7.q_ref.refs_0_ = bf16[256,512]{1,0:T(8,128)(2,1)S(1)} collective-permute-done((bf16[256,512]{1,0:T(8,128)(2,1)S(1)}, bf16[256,512]{1,0:T(8,128)(2,1)S(1)}, u32[]{:S(2)}, u32[]{:S(2)}) %collective-permute-start.7) | collective-permute-done | bytes 262176 | tf_op jit(solution)/shard_map/ppermute | solution.py:380
  32.2 0.1 collective-permute-start.15
  32.2 1.8 %shard_map.62.refs_1_.refs_0_ = s16[528,256]{1,0:T(8,128)(2,1)S(1)} custom-call(bf16[256,512]{1,0:T(8,128)(2,1)S(1)} %collective-permute-done.7.q_ref.refs_0_, bf16[1024,512]{1,0:T(8,128)(2,1)S(1)} %copy-done.1, bf16[512,1024]{1,0:T(8,128)(2,1)S(1)} %bitcast.8), custom_call_target="tpu_custom_call" | custom-call | flops 536870912 | bytes 2629632 | tf_op jit(solution)/shard_map/pallas_call | solution.py:349
  34.1 0.0 collective-permute-done.8.refs_2_.q_ref
  34.1 0.0 collective-permute-done.3.refs_2_.refs_3_
  34.1 0.0 collective-permute-done.4.refs_3_.refs_4_
  34.1 2.2 %collective-permute-done.5.refs_4_.refs_5_ = bf16[128,1024]{1,0:T(8,128)(2,1)S(1)} collective-permute-done((bf16[128,1024]{1,0:T(8,128)(2,1)}, bf16[128,1024]{1,0:T(8,128)(2,1)S(1)}, u32[]{:S(2)}, u32[]{:S(2)}) %collective-permute-start.5) | collective-permute-done | bytes 262176 | tf_op jit(solution)/shard_map/ppermute | solution.py:377
  36.3 1.5 %collective-permute-start.9 = (bf16[256,512]{1,0:T(8,128)(2,1)S(1)}, bf16[256,512]{1,0:T(8,128)(2,1)S(1)}, u32[]{:S(2)}, u32[]{:S(2)}) collective-permute-start(bf16[256,512]{1,0:T(8,128)(2,1)S(1)} %shard_map.63), channel_id=1, source_target_pairs={{0,4},{4,0},{8,12},{12,8},{1,5},{5,1},{9,13},{13,9},{2,6},{6,2},{1... | collective-permute-start | bytes 786440 | tf_op jit(solution)/shard_map/ppermute | solution.py:380
  37.8 3.5 %collective-permute-done.15.q_ref = bf16[256,512]{1,0:T(8,128)(2,1)S(1)} collective-permute-done((bf16[256,512]{1,0:T(8,128)(2,1)S(1)}, bf16[256,512]{1,0:T(8,128)(2,1)S(1)}, u32[]{:S(2)}, u32[]{:S(2)}) %collective-permute-start.15) | collective-permute-done | bytes 262176 | tf_op jit(solution)/shard_map/ppermute | solution.py:380
  41.3 1.8 %shard_map.71 = s16[528,256]{1,0:T(8,128)(2,1)S(1)} custom-call(bf16[256,512]{1,0:T(8,128)(2,1)S(1)} %collective-permute-done.15.q_ref, bf16[1024,512]{1,0:T(8,128)(2,1)S(1)} %copy-done.1, bf16[512,1024]{1,0:T(8,128)(2,1)S(1)} %bitcast.9), custom_call_target="tpu_custom_call" | custom-call | flops 536870912 | bytes 2629632 | tf_op jit(solution)/shard_map/pallas_call | solution.py:349
  43.1 0.1 collective-permute-start.16
  43.2 3.7 %collective-permute-done.9.q_ref = bf16[256,512]{1,0:T(8,128)(2,1)S(1)} collective-permute-done((bf16[256,512]{1,0:T(8,128)(2,1)S(1)}, bf16[256,512]{1,0:T(8,128)(2,1)S(1)}, u32[]{:S(2)}, u32[]{:S(2)}) %collective-permute-start.9) | collective-permute-done | bytes 262176 | tf_op jit(solution)/shard_map/ppermute | solution.py:380
  46.9 1.8 %shard_map.64 = s16[528,256]{1,0:T(8,128)(2,1)S(1)} custom-call(bf16[256,512]{1,0:T(8,128)(2,1)S(1)} %collective-permute-done.9.q_ref, bf16[1024,512]{1,0:T(8,128)(2,1)S(1)} %copy-done.1, bf16[512,1024]{1,0:T(8,128)(2,1)S(1)} %bitcast.10), custom_call_target="tpu_custom_call" | custom-call | flops 536870912 | bytes 2629632 | tf_op jit(solution)/shard_map/pallas_call | solution.py:349
  48.8 0.2 collective-permute-start.10
  48.9 1.8 %shard_map.73.refs_0_ = s16[528,256]{1,0:T(8,128)(2,1)S(1)} custom-call(bf16[256,512]{1,0:T(8,128)(2,1)S(1)} %collective-permute-done.8.refs_2_.q_ref, bf16[1024,512]{1,0:T(8,128)(2,1)S(1)} %copy-done.1, bf16[512,1024]{1,0:T(8,128)(2,1)S(1)} %bitcast.11), custom_call_target="tpu_custom_call" | custom-call | flops 536870912 | bytes 2629632 | tf_op jit(solution)/shard_map/pallas_call | solution.py:349
  50.7 2.0 %collective-permute-done.16.refs_1_ = s16[528,256]{1,0:T(8,128)(2,1)S(1)} collective-permute-done((s16[528,256]{1,0:T(8,128)(2,1)S(1)}, s16[528,256]{1,0:T(8,128)(2,1)S(1)}, u32[]{:S(2)}, u32[]{:S(2)}) %collective-permute-start.16) | collective-permute-done | bytes 270368 | tf_op jit(solution)/shard_map/ppermute | solution.py:380
  52.7 0.2 shard_map.72.refs_1_
  53.0 0.2 collective-permute-start.18
  53.2 2.6 %collective-permute-start.17 = (s16[528,256]{1,0:T(8,128)(2,1)S(1)}, s16[528,256]{1,0:T(8,128)(2,1)S(1)}, u32[]{:S(2)}, u32[]{:S(2)}) collective-permute-start(s16[528,256]{1,0:T(8,128)(2,1)S(1)} %shard_map.72.refs_1_), channel_id=1, source_target_pairs={{0,8},{4,12},{8,0},{12,4},{1,9},{5,13},{9,1},{13,5},{2,10},{6,14},... | collective-permute-start | bytes 811016 | tf_op jit(solution)/shard_map/ppermute | solution.py:380
  55.7 8.6 %collective-permute-done.10.refs_1_ = s16[528,256]{1,0:T(8,128)(2,1)S(1)} collective-permute-done((s16[528,256]{1,0:T(8,128)(2,1)S(1)}, s16[528,256]{1,0:T(8,128)(2,1)S(1)}, u32[]{:S(2)}, u32[]{:S(2)}) %collective-permute-start.10) | collective-permute-done | bytes 270368 | tf_op jit(solution)/shard_map/ppermute | solution.py:380
  64.3 0.2 shard_map.65.refs_1_
  64.6 0.0 copy-start.3
  64.6 0.1 collective-permute-start.13
  64.7 2.7 %collective-permute-start.11 = (s16[528,256]{1,0:T(8,128)(2,1)S(1)}, s16[528,256]{1,0:T(8,128)(2,1)S(1)}, u32[]{:S(2)}, u32[]{:S(2)}) collective-permute-start(s16[528,256]{1,0:T(8,128)(2,1)S(1)} %shard_map.65.refs_1_), channel_id=1, source_target_pairs={{0,8},{4,12},{8,0},{12,4},{1,9},{5,13},{9,1},{13,5},{2,10},{6,14},... | collective-permute-start | bytes 811016 | tf_op jit(solution)/shard_map/ppermute | solution.py:380
  67.4 3.4 %shard_map.69.refs_0_ = s16[528,256]{1,0:T(8,128)(2,1)S(1)} custom-call(s32[4]{0:T(128)S(1)} %copy-done.8, bf16[256,512]{1,0:T(8,128)(2,1)S(1)} %copy-done.3, bf16[128,1024]{1,0:T(8,128)(2,1)S(1)} %copy-done.6, bf16[128,1024]{1,0:T(8,128)(2,1)S(1)} %collective-permute-done.3.refs_2_.refs_3_, bf16[128,1024]{1,0:T(8,128)(2,1)S(1)} %collective-permute-done.4.refs_3_.refs_4_, ...), custom_call_target="tpu_custom_call" | custom-call | flops 805306368 | bytes 3678208 | tf_op jit(solution)/shard_map/pallas_call | solution.py:349
  70.8 3.3 %shard_map.60.refs_0_ = s16[528,256]{1,0:T(8,128)(2,1)S(1)} custom-call(s32[4]{0:T(128)S(1)} %copy-done.8, bf16[256,512]{1,0:T(8,128)(2,1)S(1)} %shard_map.56.refs_0_, bf16[128,1024]{1,0:T(8,128)(2,1)S(1)} %copy-done.6, bf16[128,1024]{1,0:T(8,128)(2,1)S(1)} %collective-permute-done.3.refs_2_.refs_3_, ...), custom_call_target="tpu_custom_call" | custom-call | flops 805306368 | bytes 3678208 | tf_op jit(solution)/shard_map/pallas_call | solution.py:349
  74.1 0.0 collective-permute-done.18.refs_2_
  74.1 0.0 collective-permute-done.17.refs_1_
  74.1 0.3 shard_map.75
  74.4 2.2 %collective-permute-start.19 = (bf16[128,512]{1,0:T(8,128)(2,1)S(1)}, bf16[128,512]{1,0:T(8,128)(2,1)S(1)}, u32[]{:S(2)}, u32[]{:S(2)}) collective-permute-start(bf16[128,512]{1,0:T(8,128)(2,1)S(1)} %get-tuple-element.27), channel_id=1, source_target_pairs={{0,2},{1,3},{2,0},{3,1},{4,6},{5,7},{6,4},{7,5},{8,10},{9,11},{10,... | collective-permute-start | bytes 393224 | tf_op jit(solution)/shard_map/ppermute | solution.py:377
  76.5 0.0 collective-permute-start.20
  76.6 4.9 %collective-permute-done.13.refs_2_ = s16[528,256]{1,0:T(8,128)(2,1)S(1)} collective-permute-done((s16[528,256]{1,0:T(8,128)(2,1)S(1)}, s16[528,256]{1,0:T(8,128)(2,1)S(1)}, u32[]{:S(2)}, u32[]{:S(2)}) %collective-permute-start.13) | collective-permute-done | bytes 270368 | tf_op jit(solution)/shard_map/ppermute | solution.py:380
  81.4 0.0 collective-permute-done.11.refs_1_
  81.4 0.3 shard_map.68
  81.7 0.1 collective-permute-start.14
  81.8 0.0 collective-permute-done.19.refs_2_
  81.8 1.2 %collective-permute-done.20.refs_3_ = bf16[128,512]{1,0:T(8,128)(2,1)S(1)} collective-permute-done((bf16[128,512]{1,0:T(8,128)(2,1)S(1)}, bf16[128,512]{1,0:T(8,128)(2,1)S(1)}, u32[]{:S(2)}, u32[]{:S(2)}) %collective-permute-start.20) | collective-permute-done | bytes 131104 | tf_op jit(solution)/shard_map/ppermute | solution.py:377
  83.1 0.1 collective-permute-done.14.refs_1_
  83.1 1.4 %shard_map.76 = bf16[128,2048]{1,0:T(8,128)(2,1)} custom-call(s32[4]{0:T(128)S(1)} %copy-done.8, bf16[128,512]{1,0:T(8,128)(2,1)S(1)} %get-tuple-element.25.refs_0_, bf16[128,512]{1,0:T(8,128)(2,1)S(1)} %collective-permute-done.14.refs_1_, bf16[128,512]{1,0:T(8,128)(2,1)S(1)} %collective-permute-done.19.refs_2_, ...), custom_call_target="tpu_custom_call" | custom-call | bytes 1048576 | tf_op jit(solution)/shard_map/pallas_call | solution.py:349
  (22 shorter events, 0.1 us)
Async XLA Ops:
  0.1 1.0 %copy-start.4 = (bf16[128,2048]{1,0:T(8,128)(2,1)S(1)}, bf16[128,2048]{1,0:T(8,128)(2,1)}, u32[]{:S(2)}) copy-start(bf16[128,2048]{1,0:T(8,128)(2,1)} %ref.3) | copy-start | bytes 1572868
  1.1 7.7 %copy-start.7 = (s32[4]{0:T(128)}, s32[4]{0:T(128)S(1)}, u32[]{:S(2)}) copy-start(s32[4]{0:T(128)S(1)} %pad_add_fusion.order_ref.refs_0_) | copy-start | bytes 52
  1.1 7.7 %copy-start.5 = (bf16[128,2048]{1,0:T(8,128)(2,1)S(1)}, bf16[128,2048]{1,0:T(8,128)(2,1)}, u32[]{:S(2)}) copy-start(bf16[128,2048]{1,0:T(8,128)(2,1)} %ref.3) | copy-start | bytes 1572868
  1.1 16.0 %copy-start.9 = (bf16[1024,512]{1,0:T(8,128)(2,1)S(1)}, bf16[1024,512]{1,0:T(8,128)(2,1)}, u32[]{:S(2)}) copy-start(bf16[1024,512]{1,0:T(8,128)(2,1)} %param.10) | copy-start | bytes 3145732
  1.7 1.5 %collective-permute-start = (bf16[128,512]{1,0:T(8,128)(2,1)S(1)}, bf16[128,512]{1,0:T(8,128)(2,1)S(1)}, u32[]{:S(2)}, u32[]{:S(2)}) collective-permute-start(bf16[128,512]{1,0:T(8,128)(2,1)S(1)} %get-tuple-element.18), channel_id=1, source_target_pairs={{0,1},{1,0},{2,3},{3,2},{4,5},{5,4},{6,7},{7,6},{8,9},{9,8},{10,11... | collective-permute-start | bytes 393224 | tf_op jit(solution)/shard_map/ppermute | solution.py:377
  3.2 19.1 %collective-permute-start.12 = (bf16[256,512]{1,0:T(8,128)(2,1)S(1)}, bf16[256,512]{1,0:T(8,128)(2,1)}, u32[]{:S(2)}, u32[]{:S(2)}) collective-permute-start(bf16[256,512]{1,0:T(8,128)(2,1)S(1)} %shard_map.56.refs_0_), channel_id=1, source_target_pairs={{0,4},{4,0},{8,12},{12,8},{1,5},{5,1},{9,13},{13,9},{2,6},{6,2},{1... | collective-permute-start | bytes 786440 | tf_op jit(solution)/shard_map/ppermute | solution.py:380
  6.2 19.9 %collective-permute-start.6 = (bf16[256,512]{1,0:T(8,128)(2,1)S(1)}, bf16[256,512]{1,0:T(8,128)(2,1)S(1)}, u32[]{:S(2)}, u32[]{:S(2)}) collective-permute-start(bf16[256,512]{1,0:T(8,128)(2,1)S(1)} %shard_map.56.refs_0_), channel_id=1, source_target_pairs={{0,8},{4,12},{8,0},{12,4},{1,9},{5,13},{9,1},{13,5},{2,10},{6,14},... | collective-permute-start | bytes 786440 | tf_op jit(solution)/shard_map/ppermute | solution.py:380
  9.4 5.6 %collective-permute-start.1 = (bf16[128,512]{1,0:T(8,128)(2,1)S(1)}, bf16[128,512]{1,0:T(8,128)(2,1)S(1)}, u32[]{:S(2)}, u32[]{:S(2)}) collective-permute-start(bf16[128,512]{1,0:T(8,128)(2,1)S(1)} %get-tuple-element.19), channel_id=1, source_target_pairs={{0,2},{1,3},{2,0},{3,1},{4,6},{5,7},{6,4},{7,5},{8,10},{9,11},{10,... | collective-permute-start | bytes 393224 | tf_op jit(solution)/shard_map/ppermute | solution.py:377
  10.9 5.8 %collective-permute-start.2 = (bf16[128,512]{1,0:T(8,128)(2,1)S(1)}, bf16[128,512]{1,0:T(8,128)(2,1)S(1)}, u32[]{:S(2)}, u32[]{:S(2)}) collective-permute-start(bf16[128,512]{1,0:T(8,128)(2,1)S(1)} %get-tuple-element.20), channel_id=1, source_target_pairs={{0,3},{1,2},{2,1},{3,0},{4,7},{5,6},{6,5},{7,4},{8,11},{9,10},{10,... | collective-permute-start | bytes 393224 | tf_op jit(solution)/shard_map/ppermute | solution.py:377
  16.7 1.7 %copy-start.2 = (bf16[256,512]{1,0:T(8,128)(2,1)}, bf16[256,512]{1,0:T(8,128)(2,1)S(1)}, u32[]{:S(2)}) copy-start(bf16[256,512]{1,0:T(8,128)(2,1)S(1)} %shard_map.58.refs_3_.refs_0_) | copy-start | bytes 786436
  16.8 15.4 %collective-permute-start.7 = (bf16[256,512]{1,0:T(8,128)(2,1)S(1)}, bf16[256,512]{1,0:T(8,128)(2,1)S(1)}, u32[]{:S(2)}, u32[]{:S(2)}) collective-permute-start(bf16[256,512]{1,0:T(8,128)(2,1)S(1)} %shard_map.58.refs_3_.refs_0_), channel_id=1, source_target_pairs={{0,8},{4,12},{8,0},{12,4},{1,9},{5,13},{9,1},{13,5},{2,10},{6,14},... | collective-permute-start | bytes 786440 | tf_op jit(solution)/shard_map/ppermute | solution.py:380
  18.5 15.6 %collective-permute-start.8 = (bf16[256,512]{1,0:T(8,128)(2,1)S(1)}, bf16[256,512]{1,0:T(8,128)(2,1)S(1)}, u32[]{:S(2)}, u32[]{:S(2)}) collective-permute-start(bf16[256,512]{1,0:T(8,128)(2,1)S(1)} %shard_map.58.refs_3_.refs_0_), channel_id=1, source_target_pairs={{0,4},{4,0},{8,12},{12,8},{1,5},{5,1},{9,13},{13,9},{2,6},{6,2},{1... | collective-permute-start | bytes 786440 | tf_op jit(solution)/shard_map/ppermute | solution.py:380
  19.0 7.2 %copy-start = (bf16[1024,512]{0,1:T(8,128)(2,1)S(1)}, bf16[1024,512]{0,1:T(8,128)(2,1)}, u32[]{:S(2)}) copy-start(bf16[1024,512]{0,1:T(8,128)(2,1)} %copy.6) | copy-start | bytes 3145732
  19.0 7.2 %copy-start.1 = (bf16[1024,512]{1,0:T(8,128)(2,1)S(1)}, bf16[1024,512]{1,0:T(8,128)(2,1)}, u32[]{:S(2)}) copy-start(bf16[1024,512]{1,0:T(8,128)(2,1)} %ck_ref.11) | copy-start | bytes 3145732
  22.2 11.9 %collective-permute-start.3 = (bf16[128,1024]{1,0:T(8,128)(2,1)}, bf16[128,1024]{1,0:T(8,128)(2,1)S(1)}, u32[]{:S(2)}, u32[]{:S(2)}) collective-permute-start(bf16[128,1024]{1,0:T(8,128)(2,1)} %get-tuple-element.22), channel_id=1, source_target_pairs={{0,1},{1,0},{2,3},{3,2},{4,5},{5,4},{6,7},{7,6},{8,9},{9,8},{10,11... | collective-permute-start | bytes 786440 | tf_op jit(solution)/shard_map/ppermute | solution.py:377
  22.3 11.8 %collective-permute-start.4 = (bf16[128,1024]{1,0:T(8,128)(2,1)}, bf16[128,1024]{1,0:T(8,128)(2,1)S(1)}, u32[]{:S(2)}, u32[]{:S(2)}) collective-permute-start(bf16[128,1024]{1,0:T(8,128)(2,1)} %get-tuple-element.23), channel_id=1, source_target_pairs={{0,2},{1,3},{2,0},{3,1},{4,6},{5,7},{6,4},{7,5},{8,10},{9,11},{10,... | collective-permute-start | bytes 786440 | tf_op jit(solution)/shard_map/ppermute | solution.py:377
  26.2 10.2 %collective-permute-start.5 = (bf16[128,1024]{1,0:T(8,128)(2,1)}, bf16[128,1024]{1,0:T(8,128)(2,1)S(1)}, u32[]{:S(2)}, u32[]{:S(2)}) collective-permute-start(bf16[128,1024]{1,0:T(8,128)(2,1)} %get-tuple-element.24), channel_id=1, source_target_pairs={{0,3},{1,2},{2,1},{3,0},{4,7},{5,6},{6,5},{7,4},{8,11},{9,10},{10,... | collective-permute-start | bytes 786440 | tf_op jit(solution)/shard_map/ppermute | solution.py:377
  32.2 9.2 %collective-permute-start.15 = (bf16[256,512]{1,0:T(8,128)(2,1)S(1)}, bf16[256,512]{1,0:T(8,128)(2,1)S(1)}, u32[]{:S(2)}, u32[]{:S(2)}) collective-permute-start(bf16[256,512]{1,0:T(8,128)(2,1)S(1)} %shard_map.70), channel_id=1, source_target_pairs={{0,4},{4,0},{8,12},{12,8},{1,5},{5,1},{9,13},{13,9},{2,6},{6,2},{1... | collective-permute-start | bytes 786440 | tf_op jit(solution)/shard_map/ppermute | solution.py:380
  36.3 10.6 %collective-permute-start.9 = (bf16[256,512]{1,0:T(8,128)(2,1)S(1)}, bf16[256,512]{1,0:T(8,128)(2,1)S(1)}, u32[]{:S(2)}, u32[]{:S(2)}) collective-permute-start(bf16[256,512]{1,0:T(8,128)(2,1)S(1)} %shard_map.63), channel_id=1, source_target_pairs={{0,4},{4,0},{8,12},{12,8},{1,5},{5,1},{9,13},{13,9},{2,6},{6,2},{1... | collective-permute-start | bytes 786440 | tf_op jit(solution)/shard_map/ppermute | solution.py:380
  43.1 9.6 %collective-permute-start.16 = (s16[528,256]{1,0:T(8,128)(2,1)S(1)}, s16[528,256]{1,0:T(8,128)(2,1)S(1)}, u32[]{:S(2)}, u32[]{:S(2)}) collective-permute-start(s16[528,256]{1,0:T(8,128)(2,1)S(1)} %shard_map.71), channel_id=1, source_target_pairs={{0,4},{4,0},{8,12},{12,8},{1,5},{5,1},{9,13},{13,9},{2,6},{6,2},{1... | collective-permute-start | bytes 811016 | tf_op jit(solution)/shard_map/ppermute | solution.py:380
  48.8 15.6 %collective-permute-start.10 = (s16[528,256]{1,0:T(8,128)(2,1)S(1)}, s16[528,256]{1,0:T(8,128)(2,1)S(1)}, u32[]{:S(2)}, u32[]{:S(2)}) collective-permute-start(s16[528,256]{1,0:T(8,128)(2,1)S(1)} %shard_map.64), channel_id=1, source_target_pairs={{0,4},{4,0},{8,12},{12,8},{1,5},{5,1},{9,13},{13,9},{2,6},{6,2},{1... | collective-permute-start | bytes 811016 | tf_op jit(solution)/shard_map/ppermute | solution.py:380
  53.0 21.1 %collective-permute-start.18 = (s16[528,256]{1,0:T(8,128)(2,1)S(1)}, s16[528,256]{1,0:T(8,128)(2,1)S(1)}, u32[]{:S(2)}, u32[]{:S(2)}) collective-permute-start(s16[528,256]{1,0:T(8,128)(2,1)S(1)} %shard_map.74), channel_id=1, source_target_pairs={{0,4},{4,0},{8,12},{12,8},{1,5},{5,1},{9,13},{13,9},{2,6},{6,2},{1... | collective-permute-start | bytes 811016 | tf_op jit(solution)/shard_map/ppermute | solution.py:380
  53.2 20.9 %collective-permute-start.17 = (s16[528,256]{1,0:T(8,128)(2,1)S(1)}, s16[528,256]{1,0:T(8,128)(2,1)S(1)}, u32[]{:S(2)}, u32[]{:S(2)}) collective-permute-start(s16[528,256]{1,0:T(8,128)(2,1)S(1)} %shard_map.72.refs_1_), channel_id=1, source_target_pairs={{0,8},{4,12},{8,0},{12,4},{1,9},{5,13},{9,1},{13,5},{2,10},{6,14},... | collective-permute-start | bytes 811016 | tf_op jit(solution)/shard_map/ppermute | solution.py:380
  64.6 2.8 %copy-start.3 = (bf16[256,512]{1,0:T(8,128)(2,1)S(1)}, bf16[256,512]{1,0:T(8,128)(2,1)}, u32[]{:S(2)}) copy-start(bf16[256,512]{1,0:T(8,128)(2,1)} %copy-done.2) | copy-start | bytes 786436
  64.6 2.8 %copy-start.6 = (bf16[128,1024]{1,0:T(8,128)(2,1)S(1)}, bf16[128,1024]{1,0:T(8,128)(2,1)}, u32[]{:S(2)}) copy-start(bf16[128,1024]{1,0:T(8,128)(2,1)} %get-tuple-element.21.refs_1_) | copy-start | bytes 786436
  64.6 2.7 %copy-start.8 = (s32[4]{0:T(128)S(1)}, s32[4]{0:T(128)}, u32[]{:S(2)}) copy-start(s32[4]{0:T(128)} %copy-done.7) | copy-start | bytes 52
  64.6 16.8 %collective-permute-start.13 = (s16[528,256]{1,0:T(8,128)(2,1)S(1)}, s16[528,256]{1,0:T(8,128)(2,1)S(1)}, u32[]{:S(2)}, u32[]{:S(2)}) collective-permute-start(s16[528,256]{1,0:T(8,128)(2,1)S(1)} %shard_map.67), channel_id=1, source_target_pairs={{0,4},{4,0},{8,12},{12,8},{1,5},{5,1},{9,13},{13,9},{2,6},{6,2},{1... | collective-permute-start | bytes 811016 | tf_op jit(solution)/shard_map/ppermute | solution.py:380
  64.7 16.7 %collective-permute-start.11 = (s16[528,256]{1,0:T(8,128)(2,1)S(1)}, s16[528,256]{1,0:T(8,128)(2,1)S(1)}, u32[]{:S(2)}, u32[]{:S(2)}) collective-permute-start(s16[528,256]{1,0:T(8,128)(2,1)S(1)} %shard_map.65.refs_1_), channel_id=1, source_target_pairs={{0,8},{4,12},{8,0},{12,4},{1,9},{5,13},{9,1},{13,5},{2,10},{6,14},... | collective-permute-start | bytes 811016 | tf_op jit(solution)/shard_map/ppermute | solution.py:380
  74.4 7.4 %collective-permute-start.19 = (bf16[128,512]{1,0:T(8,128)(2,1)S(1)}, bf16[128,512]{1,0:T(8,128)(2,1)S(1)}, u32[]{:S(2)}, u32[]{:S(2)}) collective-permute-start(bf16[128,512]{1,0:T(8,128)(2,1)S(1)} %get-tuple-element.27), channel_id=1, source_target_pairs={{0,2},{1,3},{2,0},{3,1},{4,6},{5,7},{6,4},{7,5},{8,10},{9,11},{10,... | collective-permute-start | bytes 393224 | tf_op jit(solution)/shard_map/ppermute | solution.py:377
  76.5 6.5 %collective-permute-start.20 = (bf16[128,512]{1,0:T(8,128)(2,1)S(1)}, bf16[128,512]{1,0:T(8,128)(2,1)S(1)}, u32[]{:S(2)}, u32[]{:S(2)}) collective-permute-start(bf16[128,512]{1,0:T(8,128)(2,1)S(1)} %get-tuple-element.28), channel_id=1, source_target_pairs={{0,3},{1,2},{2,1},{3,0},{4,7},{5,6},{6,5},{7,4},{8,11},{9,10},{10,... | collective-permute-start | bytes 393224 | tf_op jit(solution)/shard_map/ppermute | solution.py:377
  81.7 1.4 %collective-permute-start.14 = (bf16[128,512]{1,0:T(8,128)(2,1)S(1)}, bf16[128,512]{1,0:T(8,128)(2,1)S(1)}, u32[]{:S(2)}, u32[]{:S(2)}) collective-permute-start(bf16[128,512]{1,0:T(8,128)(2,1)S(1)} %get-tuple-element.26), channel_id=1, source_target_pairs={{0,1},{1,0},{2,3},{3,2},{4,5},{5,4},{6,7},{7,6},{8,9},{9,8},{10,11... | collective-permute-start | bytes 393224 | tf_op jit(solution)/shard_map/ppermute | solution.py:377
where the time goes:
time: 84.7 us; the launch traced here: 84.5 us
  waiting for transfers between devices  36.7 us (43%)
  Pallas kernels  25.3 us (30%)
  starting transfers between devices  19.7 us (23%)
  local copies, waits for them, and re-layouts  2.4 us (3%)
    ppermute x12, waiting for transfers between devices, along(): return lax.ppermute(x, 'seq', [(i, i ^ bit) for i in range(seq_count)])  26.4 us
    pallas_call x21, Pallas kernels, call(): pl.pallas_call(kernel, out_shape=outs, in_specs=[pl.BlockSpec(memory_spac...  22.2 us
    ppermute x12, starting transfers between devices, along(): return lax.ppermute(x, 'seq', [(i, i ^ bit) for i in range(seq_count)])  13.7 us
    ppermute x9, waiting for transfers between devices, swap(): lax.ppermute(x, ('heads', 'sub'), [(i, i ^ d) for i in range(shares)])  10.3 us
    ppermute x9, starting transfers between devices, swap(): lax.ppermute(x, ('heads', 'sub'), [(i, i ^ d) for i in range(shares)])  5.99 us
    pallas_call x1, Pallas kernels, move(): pl.pallas_call(without_unread, out_shape=outs, in_specs=[pl.BlockSpec(mem...  3.14 us
    unnamed x21, local copies, waits for them, and re-layouts  2.4 us
  transfers between devices with their start and end apart: 21, of which 13 were waited for; matrix products, arithmetic and copies ran while one was open for 2% of the time, Pallas kernels for 28%

commit v1 on v0

--- a/solution.py
+++ b/solution.py
@@ -423,12 +423,12 @@
     q = slices(pieces_b)
     a2, a1 = along(a, 2), along(a, 1)
     q = [swap(x, d) for x, d in zip(q, pieces_b)]
-    b = call(functools.partial(stack_kernel, each), q, [chunk])[0]
+    kv = pick([new_keys, new_values], range(shares), pair)
+    b = call(functools.partial(stack_kernel, each), q, [chunk], unread=[kv[0], cache_vt])[0]
     b2, b1 = along(b, 2), along(b, 1)
-    kv = pick([new_keys, new_values], range(shares), pair, [b, cache_vt])
-    kv = [swap(x, d) if d else x for d, x in enumerate(kv)]
+    kv = [swap(after(x, [b]), d) if d else x for d, x in enumerate(kv)]
     part_a2, part_a1 = attend(a2), attend(a1)
-    b3 = along(after(b2, [part_a2, part_a1]), 1)
+    b3 = along(after(b2, [part_a2, part_a1, b1]), 1)
     part_b2 = attend(b2)
     a3 = along(after(a2, [part_b2, b1, *kv[1:]]), 1)
     got_b2 = along(attend(b3), 1)

time: 84.7 us -> 86.4 us (1.020)
  waiting for transfers between devices: 36.7 us -> 40.7 us
  starting transfers between devices: 19.7 us -> 16.4 us
  local copies, waits for them, and re-layouts: 2.4 us -> 3.63 us
    ppermute x12, waiting for transfers between devices: 26.4 us -> 35.2 us  [along(): return lax.ppermute(x, 'seq', [(i, i ^ bit) for i in range(seq_count)])]
    ppermute x9, waiting for transfers between devices: 10.3 us -> 5.59 us  [swap(): lax.ppermute(x, ('heads', 'sub'), [(i, i ^ d) for i in range(shares)])]
    ppermute x12, starting transfers between devices: 13.7 us -> 11 us  [along(): return lax.ppermute(x, 'seq', [(i, i ^ bit) for i in range(seq_count)])]
    unnamed x21 -> x23, local copies, waits for them, and re-layouts: 2.4 us -> 3.63 us
    pallas_call x21 -> x24, Pallas kernels: 22.2 us -> 21.6 us  [call(): pl.pallas_call(kernel, out_shape=outs, in_specs=[pl.BlockSpec(memory_spac...]
  transfers between devices with their start and end apart: 21 -> 21, of which waited for: 13 -> 13; matrix products, arithmetic and copies ran while one was open for 2% -> 1% of each run, Pallas kernels for 28% -> 26%
where the time goes in v1:
time: 86.4 us; the launch traced here: 85.7 us
  waiting for transfers between devices  40.7 us (47%)
  Pallas kernels  24.6 us (28%)
  starting transfers between devices  16.4 us (19%)
  local copies, waits for them, and re-layouts  3.63 us (4%)
    ppermute x12, waiting for transfers between devices, along(): return lax.ppermute(x, 'seq', [(i, i ^ bit) for i in range(seq_count)])  35.2 us
    pallas_call x24, Pallas kernels, call(): pl.pallas_call(kernel, out_shape=outs, in_specs=[pl.BlockSpec(memory_spac...  21.6 us
    ppermute x12, starting transfers between devices, along(): return lax.ppermute(x, 'seq', [(i, i ^ bit) for i in range(seq_count)])  11 us
    ppermute x9, waiting for transfers between devices, swap(): lax.ppermute(x, ('heads', 'sub'), [(i, i ^ d) for i in range(shares)])  5.59 us
    ppermute x9, starting transfers between devices, swap(): lax.ppermute(x, ('heads', 'sub'), [(i, i ^ d) for i in range(shares)])  5.44 us
    unnamed x23, local copies, waits for them, and re-layouts  3.63 us
    pallas_call x1, Pallas kernels, move(): pl.pallas_call(without_unread, out_shape=outs, in_specs=[pl.BlockSpec(mem...  2.98 us
  transfers between devices with their start and end apart: 21, of which 13 were waited for; matrix products, arithmetic and copies ran while one was open for 1% of the time, Pallas kernels for 26%

profile of v1, /device:TPU:0, one launch (start us, length us, event | category | flops | bytes accessed | tf_op | source)
XLA Modules:
  0.0 85.7 jit_solution(6421394278287374256)
XLA Ops:
  0.0 0.1 pad_add_fusion.order_ref.refs_0_
  0.1 1.0 %copy-done.3 = bf16[128,2048]{1,0:T(8,128)(2,1)S(1)} copy-done((bf16[128,2048]{1,0:T(8,128)(2,1)S(1)}, bf16[128,2048]{1,0:T(8,128)(2,1)}, u32[]{:S(2)}) %copy-start.3) | copy-done | bytes 524312
  1.1 0.6 shard_map.55
  1.7 0.5 collective-permute-start
  2.2 1.0 %collective-permute-done.refs_1_ = bf16[128,512]{1,0:T(8,128)(2,1)S(1)} collective-permute-done((bf16[128,512]{1,0:T(8,128)(2,1)S(1)}, bf16[128,512]{1,0:T(8,128)(2,1)S(1)}, u32[]{:S(2)}, u32[]{:S(2)}) %collective-permute-start) | collective-permute-done | bytes 131104 | tf_op jit(solution)/shard_map/ppermute | solution.py:377
  3.2 3.0 %collective-permute-start.12 = (bf16[256,512]{1,0:T(8,128)(2,1)S(1)}, bf16[256,512]{1,0:T(8,128)(2,1)S(1)}, u32[]{:S(2)}, u32[]{:S(2)}) collective-permute-start(bf16[256,512]{1,0:T(8,128)(2,1)S(1)} %shard_map.56.refs_0_), channel_id=1, source_target_pairs={{0,4},{4,0},{8,12},{12,8},{1,5},{5,1},{9,13},{13,9},{2,6},{6,2},{1... | collective-permute-start | bytes 786440 | tf_op jit(solution)/shard_map/ppermute | solution.py:380
  6.2 2.6 %collective-permute-start.6 = (bf16[256,512]{1,0:T(8,128)(2,1)S(1)}, bf16[256,512]{1,0:T(8,128)(2,1)S(1)}, u32[]{:S(2)}, u32[]{:S(2)}) collective-permute-start(bf16[256,512]{1,0:T(8,128)(2,1)S(1)} %shard_map.56.refs_0_), channel_id=1, source_target_pairs={{0,8},{4,12},{8,0},{12,4},{1,9},{5,13},{9,1},{13,5},{2,10},{6,14},... | collective-permute-start | bytes 786440 | tf_op jit(solution)/shard_map/ppermute | solution.py:380
  8.8 0.6 shard_map.58
  9.4 1.6 %collective-permute-start.1 = (bf16[128,512]{1,0:T(8,128)(2,1)S(1)}, bf16[128,512]{1,0:T(8,128)(2,1)S(1)}, u32[]{:S(2)}, u32[]{:S(2)}) collective-permute-start(bf16[128,512]{1,0:T(8,128)(2,1)S(1)} %get-tuple-element.21), channel_id=1, source_target_pairs={{0,2},{1,3},{2,0},{3,1},{4,6},{5,7},{6,4},{7,5},{8,10},{9,11},{10,... | collective-permute-start | bytes 393224 | tf_op jit(solution)/shard_map/ppermute | solution.py:377
  10.9 0.0 collective-permute-start.2
  11.0 0.5 copy.6
  11.5 3.0 %shard_map.57 = (bf16[128,1024]{1,0:T(8,128)(2,1)}, bf16[128,1024]{1,0:T(8,128)(2,1)}, bf16[128,1024]{1,0:T(8,128)(2,1)}, bf16[128,1024]{1,0:T(8,128)(2,1)}) custom-call(s32[4]{0:T(128)} %copy-done.8, bf16[128,2048]{1,0:T(8,128)(2,1)} %refs_1_.1, bf16[128,2048]{1,0:T(8,128)(2,1)} %refs_2_.1), custom_call_target="tpu_custom_call" | custom-call | bytes 1048576 | tf_op jit(solution)/shard_map/pallas_call | solution.py:334
  14.5 0.5 collective-permute-done.1.refs_0_
  15.0 1.8 %collective-permute-done.2.refs_1_ = bf16[128,512]{1,0:T(8,128)(2,1)S(1)} collective-permute-done((bf16[128,512]{1,0:T(8,128)(2,1)S(1)}, bf16[128,512]{1,0:T(8,128)(2,1)S(1)}, u32[]{:S(2)}, u32[]{:S(2)}) %collective-permute-start.2) | collective-permute-done | bytes 131104 | tf_op jit(solution)/shard_map/ppermute | solution.py:377
  16.7 0.9 %copy-done.1 = bf16[128,1024]{1,0:T(8,128)(2,1)S(1)} copy-done((bf16[128,1024]{1,0:T(8,128)(2,1)S(1)}, bf16[128,1024]{1,0:T(8,128)(2,1)}, u32[]{:S(2)}) %copy-start.1) | copy-done | bytes 262168
  17.7 0.5 collective-permute-start.8
  18.2 0.4 collective-permute-start.7
  18.6 0.0 copy-done.7
  18.7 0.1 copy-done.6
  18.7 1.0 %copy-done.5 = bf16[128,1024]{1,0:T(8,128)(2,1)S(1)} copy-done((bf16[128,1024]{1,0:T(8,128)(2,1)S(1)}, bf16[128,1024]{1,0:T(8,128)(2,1)}, u32[]{:S(2)}) %copy-start.5) | copy-done | bytes 262168
  19.8 1.8 %collective-permute-start.5 = (bf16[128,1024]{1,0:T(8,128)(2,1)S(1)}, bf16[128,1024]{1,0:T(8,128)(2,1)S(1)}, u32[]{:S(2)}, u32[]{:S(2)}) collective-permute-start(bf16[128,1024]{1,0:T(8,128)(2,1)S(1)} %shard_map.62), channel_id=1, source_target_pairs={{0,3},{1,2},{2,1},{3,0},{4,7},{5,6},{6,5},{7,4},{8,11},{9,10},{10,... | collective-permute-start | bytes 786440 | tf_op jit(solution)/shard_map/ppermute | solution.py:377
  21.6 0.0 collective-permute-done.12.q_ref
  21.6 0.5 collective-permute-start.4
  22.1 0.0 collective-permute-done.6.q_ref.refs_0_
  22.1 0.0 collective-permute-start.3
  22.1 1.8 %shard_map.69.refs_0_.refs_2_ = s16[528,256]{1,0:T(8,128)(2,1)S(1)} custom-call(bf16[256,512]{1,0:T(8,128)(2,1)S(1)} %collective-permute-done.12.q_ref, bf16[1024,512]{1,0:T(8,128)(2,1)S(1)} %copy-done, bf16[512,1024]{1,0:T(8,128)(2,1)S(1)} %bitcast.6), custom_call_target="tpu_custom_call" | custom-call | flops 536870912 | bytes 2629632 | tf_op jit(solution)/shard_map/pallas_call | solution.py:349
  24.0 1.8 %shard_map.64.refs_0_.refs_1_ = s16[528,256]{1,0:T(8,128)(2,1)S(1)} custom-call(bf16[256,512]{1,0:T(8,128)(2,1)S(1)} %collective-permute-done.6.q_ref.refs_0_, bf16[1024,512]{1,0:T(8,128)(2,1)S(1)} %copy-done, bf16[512,1024]{1,0:T(8,128)(2,1)S(1)} %bitcast.7), custom_call_target="tpu_custom_call" | custom-call | flops 536870912 | bytes 2629632 | tf_op jit(solution)/shard_map/pallas_call | solution.py:349
  25.8 5.2 %collective-permute-done.8.refs_2_.refs_3_.q_ref = bf16[256,512]{1,0:T(8,128)(2,1)S(1)} collective-permute-done((bf16[256,512]{1,0:T(8,128)(2,1)S(1)}, bf16[256,512]{1,0:T(8,128)(2,1)S(1)}, u32[]{:S(2)}, u32[]{:S(2)}) %collective-permute-start.8) | collective-permute-done | bytes 262176 | tf_op jit(solution)/shard_map/ppermute | solution.py:380
  31.0 2.4 %collective-permute-done.7.q_ref.refs_0_ = bf16[256,512]{1,0:T(8,128)(2,1)S(1)} collective-permute-done((bf16[256,512]{1,0:T(8,128)(2,1)S(1)}, bf16[256,512]{1,0:T(8,128)(2,1)S(1)}, u32[]{:S(2)}, u32[]{:S(2)}) %collective-permute-start.7) | collective-permute-done | bytes 262176 | tf_op jit(solution)/shard_map/ppermute | solution.py:380
  33.4 0.1 collective-permute-start.15
  33.5 1.8 %shard_map.65.refs_1_.refs_0_ = s16[528,256]{1,0:T(8,128)(2,1)S(1)} custom-call(bf16[256,512]{1,0:T(8,128)(2,1)S(1)} %collective-permute-done.7.q_ref.refs_0_, bf16[1024,512]{1,0:T(8,128)(2,1)S(1)} %copy-done, bf16[512,1024]{1,0:T(8,128)(2,1)S(1)} %bitcast.8), custom_call_target="tpu_custom_call" | custom-call | flops 536870912 | bytes 2629632 | tf_op jit(solution)/shard_map/pallas_call | solution.py:349
  35.3 0.0 collective-permute-done.4.refs_3_.refs_4_
  35.3 0.0 collective-permute-done.3.refs_2_.refs_3_
  35.4 2.1 %collective-permute-start.9 = (bf16[256,512]{1,0:T(8,128)(2,1)S(1)}, bf16[256,512]{1,0:T(8,128)(2,1)S(1)}, u32[]{:S(2)}, u32[]{:S(2)}) collective-permute-start(bf16[256,512]{1,0:T(8,128)(2,1)S(1)} %shard_map.66), channel_id=1, source_target_pairs={{0,4},{4,0},{8,12},{12,8},{1,5},{5,1},{9,13},{13,9},{2,6},{6,2},{1... | collective-permute-start | bytes 786440 | tf_op jit(solution)/shard_map/ppermute | solution.py:380
  37.4 5.2 %collective-permute-done.15.q_ref = bf16[256,512]{1,0:T(8,128)(2,1)S(1)} collective-permute-done((bf16[256,512]{1,0:T(8,128)(2,1)S(1)}, bf16[256,512]{1,0:T(8,128)(2,1)S(1)}, u32[]{:S(2)}, u32[]{:S(2)}) %collective-permute-start.15) | collective-permute-done | bytes 262176 | tf_op jit(solution)/shard_map/ppermute | solution.py:380
  42.7 1.8 %shard_map.74 = s16[528,256]{1,0:T(8,128)(2,1)S(1)} custom-call(bf16[256,512]{1,0:T(8,128)(2,1)S(1)} %collective-permute-done.15.q_ref, bf16[1024,512]{1,0:T(8,128)(2,1)S(1)} %copy-done, bf16[512,1024]{1,0:T(8,128)(2,1)S(1)} %bitcast.9), custom_call_target="tpu_custom_call" | custom-call | flops 536870912 | bytes 2629632 | tf_op jit(solution)/shard_map/pallas_call | solution.py:349
  44.5 0.1 collective-permute-start.16
  44.6 3.7 %collective-permute-done.9.q_ref = bf16[256,512]{1,0:T(8,128)(2,1)S(1)} collective-permute-done((bf16[256,512]{1,0:T(8,128)(2,1)S(1)}, bf16[256,512]{1,0:T(8,128)(2,1)S(1)}, u32[]{:S(2)}, u32[]{:S(2)}) %collective-permute-start.9) | collective-permute-done | bytes 262176 | tf_op jit(solution)/shard_map/ppermute | solution.py:380
  48.3 1.8 %shard_map.67 = s16[528,256]{1,0:T(8,128)(2,1)S(1)} custom-call(bf16[256,512]{1,0:T(8,128)(2,1)S(1)} %collective-permute-done.9.q_ref, bf16[1024,512]{1,0:T(8,128)(2,1)S(1)} %copy-done, bf16[512,1024]{1,0:T(8,128)(2,1)S(1)} %bitcast.10), custom_call_target="tpu_custom_call" | custom-call | flops 536870912 | bytes 2629632 | tf_op jit(solution)/shard_map/pallas_call | solution.py:349
  50.1 0.1 collective-permute-start.10
  50.2 1.9 %shard_map.76.refs_0_ = s16[528,256]{1,0:T(8,128)(2,1)S(1)} custom-call(bf16[256,512]{1,0:T(8,128)(2,1)S(1)} %collective-permute-done.8.refs_2_.refs_3_.q_ref, bf16[1024,512]{1,0:T(8,128)(2,1)S(1)} %copy-done, bf16[512,1024]{1,0:T(8,128)(2,1)S(1)} %bitcast.11), custom_call_target="tpu_custom_call" | custom-call | flops 536870912 | bytes 2629632 | tf_op jit(solution)/shard_map/pallas_call | solution.py:349
  52.1 2.0 %collective-permute-done.16.refs_1_ = s16[528,256]{1,0:T(8,128)(2,1)S(1)} collective-permute-done((s16[528,256]{1,0:T(8,128)(2,1)S(1)}, s16[528,256]{1,0:T(8,128)(2,1)S(1)}, u32[]{:S(2)}, u32[]{:S(2)}) %collective-permute-start.16) | collective-permute-done | bytes 270368 | tf_op jit(solution)/shard_map/ppermute | solution.py:380
  54.1 0.2 shard_map.75.refs_1_
  54.3 0.1 collective-permute-start.18
  54.4 1.0 %collective-permute-start.17 = (s16[528,256]{1,0:T(8,128)(2,1)S(1)}, s16[528,256]{1,0:T(8,128)(2,1)S(1)}, u32[]{:S(2)}, u32[]{:S(2)}) collective-permute-start(s16[528,256]{1,0:T(8,128)(2,1)S(1)} %shard_map.75.refs_1_), channel_id=1, source_target_pairs={{0,8},{4,12},{8,0},{12,4},{1,9},{5,13},{9,1},{13,5},{2,10},{6,14},... | collective-permute-start | bytes 811016 | tf_op jit(solution)/shard_map/ppermute | solution.py:380
  55.5 10.2 %collective-permute-done.10.refs_1_ = s16[528,256]{1,0:T(8,128)(2,1)S(1)} collective-permute-done((s16[528,256]{1,0:T(8,128)(2,1)S(1)}, s16[528,256]{1,0:T(8,128)(2,1)S(1)}, u32[]{:S(2)}, u32[]{:S(2)}) %collective-permute-start.10) | collective-permute-done | bytes 270368 | tf_op jit(solution)/shard_map/ppermute | solution.py:380
  65.7 0.2 shard_map.68.refs_1_
  65.9 0.0 copy-start.2
  66.0 0.1 collective-permute-start.13
  66.0 1.0 %collective-permute-start.11 = (s16[528,256]{1,0:T(8,128)(2,1)S(1)}, s16[528,256]{1,0:T(8,128)(2,1)S(1)}, u32[]{:S(2)}, u32[]{:S(2)}) collective-permute-start(s16[528,256]{1,0:T(8,128)(2,1)S(1)} %shard_map.68.refs_1_), channel_id=1, source_target_pairs={{0,8},{4,12},{8,0},{12,4},{1,9},{5,13},{9,1},{13,5},{2,10},{6,14},... | collective-permute-start | bytes 811016 | tf_op jit(solution)/shard_map/ppermute | solution.py:380
  67.1 3.5 %shard_map.63.refs_0_ = s16[528,256]{1,0:T(8,128)(2,1)S(1)} custom-call(s32[4]{0:T(128)S(1)} %copy-done.9, bf16[256,512]{1,0:T(8,128)(2,1)S(1)} %shard_map.56.refs_0_, bf16[128,1024]{1,0:T(8,128)(2,1)S(1)} %copy-done.2, bf16[128,1024]{1,0:T(8,128)(2,1)S(1)} %collective-permute-done.3.refs_2_.refs_3_, ...), custom_call_target="tpu_custom_call" | custom-call | flops 805306368 | bytes 3678208 | tf_op jit(solution)/shard_map/pallas_call | solution.py:349
  70.6 3.3 %shard_map.72.refs_0_ = s16[528,256]{1,0:T(8,128)(2,1)S(1)} custom-call(s32[4]{0:T(128)S(1)} %copy-done.9, bf16[256,512]{1,0:T(8,128)(2,1)S(1)} %shard_map.59.refs_1_.refs_0_, bf16[128,1024]{1,0:T(8,128)(2,1)S(1)} %copy-done.2, bf16[128,1024]{1,0:T(8,128)(2,1)S(1)} %collective-permute-done.3.refs_2_.refs_3_, ...), custom_call_target="tpu_custom_call" | custom-call | flops 805306368 | bytes 3678208 | tf_op jit(solution)/shard_map/pallas_call | solution.py:349
  73.9 3.4 %collective-permute-done.18.refs_2_ = s16[528,256]{1,0:T(8,128)(2,1)S(1)} collective-permute-done((s16[528,256]{1,0:T(8,128)(2,1)S(1)}, s16[528,256]{1,0:T(8,128)(2,1)S(1)}, u32[]{:S(2)}, u32[]{:S(2)}) %collective-permute-start.18) | collective-permute-done | bytes 270368 | tf_op jit(solution)/shard_map/ppermute | solution.py:380
  77.3 0.0 collective-permute-done.17.refs_1_
  77.3 0.3 shard_map.78
  77.6 0.9 %collective-permute-start.19 = (bf16[128,512]{1,0:T(8,128)(2,1)S(1)}, bf16[128,512]{1,0:T(8,128)(2,1)S(1)}, u32[]{:S(2)}, u32[]{:S(2)}) collective-permute-start(bf16[128,512]{1,0:T(8,128)(2,1)S(1)} %get-tuple-element.27), channel_id=1, source_target_pairs={{0,2},{1,3},{2,0},{3,1},{4,6},{5,7},{6,4},{7,5},{8,10},{9,11},{10,... | collective-permute-start | bytes 393224 | tf_op jit(solution)/shard_map/ppermute | solution.py:377
  78.5 0.0 collective-permute-start.20
  78.5 3.1 %collective-permute-done.13.refs_2_ = s16[528,256]{1,0:T(8,128)(2,1)S(1)} collective-permute-done((s16[528,256]{1,0:T(8,128)(2,1)S(1)}, s16[528,256]{1,0:T(8,128)(2,1)S(1)}, u32[]{:S(2)}, u32[]{:S(2)}) %collective-permute-start.13) | collective-permute-done | bytes 270368 | tf_op jit(solution)/shard_map/ppermute | solution.py:380
  81.6 0.0 collective-permute-done.11.refs_1_
  81.6 0.3 shard_map.71
  81.9 0.1 collective-permute-start.14
  82.0 1.7 %collective-permute-done.19.refs_2_ = bf16[128,512]{1,0:T(8,128)(2,1)S(1)} collective-permute-done((bf16[128,512]{1,0:T(8,128)(2,1)S(1)}, bf16[128,512]{1,0:T(8,128)(2,1)S(1)}, u32[]{:S(2)}, u32[]{:S(2)}) %collective-permute-start.19) | collective-permute-done | bytes 131104 | tf_op jit(solution)/shard_map/ppermute | solution.py:377
  83.7 0.6 collective-permute-done.20.refs_3_
  84.3 1.4 %shard_map.79 = bf16[128,2048]{1,0:T(8,128)(2,1)} custom-call(s32[4]{0:T(128)S(1)} %copy-done.9, bf16[128,512]{1,0:T(8,128)(2,1)S(1)} %get-tuple-element.25.refs_0_, bf16[128,512]{1,0:T(8,128)(2,1)S(1)} %collective-permute-done.14.refs_1_, bf16[128,512]{1,0:T(8,128)(2,1)S(1)} %collective-permute-done.19.refs_2_, ...), custom_call_target="tpu_custom_call" | custom-call | bytes 1048576 | tf_op jit(solution)/shard_map/pallas_call | solution.py:349
  (27 shorter events, 0.2 us)
Async XLA Ops:
  0.1 1.0 %copy-start.3 = (bf16[128,2048]{1,0:T(8,128)(2,1)S(1)}, bf16[128,2048]{1,0:T(8,128)(2,1)}, u32[]{:S(2)}) copy-start(bf16[128,2048]{1,0:T(8,128)(2,1)} %ref.3) | copy-start | bytes 1572868
  1.1 7.7 %copy-start.8 = (s32[4]{0:T(128)}, s32[4]{0:T(128)S(1)}, u32[]{:S(2)}) copy-start(s32[4]{0:T(128)S(1)} %pad_add_fusion.order_ref.refs_0_) | copy-start | bytes 52
  1.1 7.7 %copy-start.4 = (bf16[128,2048]{1,0:T(8,128)(2,1)S(1)}, bf16[128,2048]{1,0:T(8,128)(2,1)}, u32[]{:S(2)}) copy-start(bf16[128,2048]{1,0:T(8,128)(2,1)} %ref.3) | copy-start | bytes 1572868
  1.1 9.8 %copy-start.10 = (bf16[1024,512]{1,0:T(8,128)(2,1)S(1)}, bf16[1024,512]{1,0:T(8,128)(2,1)}, u32[]{:S(2)}) copy-start(bf16[1024,512]{1,0:T(8,128)(2,1)} %param.10) | copy-start | bytes 3145732
  1.7 1.5 %collective-permute-start = (bf16[128,512]{1,0:T(8,128)(2,1)S(1)}, bf16[128,512]{1,0:T(8,128)(2,1)S(1)}, u32[]{:S(2)}, u32[]{:S(2)}) collective-permute-start(bf16[128,512]{1,0:T(8,128)(2,1)S(1)} %get-tuple-element.18), channel_id=1, source_target_pairs={{0,1},{1,0},{2,3},{3,2},{4,5},{5,4},{6,7},{7,6},{8,9},{9,8},{10,11... | collective-permute-start | bytes 393224 | tf_op jit(solution)/shard_map/ppermute | solution.py:377
  3.2 18.3 %collective-permute-start.12 = (bf16[256,512]{1,0:T(8,128)(2,1)S(1)}, bf16[256,512]{1,0:T(8,128)(2,1)S(1)}, u32[]{:S(2)}, u32[]{:S(2)}) collective-permute-start(bf16[256,512]{1,0:T(8,128)(2,1)S(1)} %shard_map.56.refs_0_), channel_id=1, source_target_pairs={{0,4},{4,0},{8,12},{12,8},{1,5},{5,1},{9,13},{13,9},{2,6},{6,2},{1... | collective-permute-start | bytes 786440 | tf_op jit(solution)/shard_map/ppermute | solution.py:380
  6.2 15.9 %collective-permute-start.6 = (bf16[256,512]{1,0:T(8,128)(2,1)S(1)}, bf16[256,512]{1,0:T(8,128)(2,1)S(1)}, u32[]{:S(2)}, u32[]{:S(2)}) collective-permute-start(bf16[256,512]{1,0:T(8,128)(2,1)S(1)} %shard_map.56.refs_0_), channel_id=1, source_target_pairs={{0,8},{4,12},{8,0},{12,4},{1,9},{5,13},{9,1},{13,5},{2,10},{6,14},... | collective-permute-start | bytes 786440 | tf_op jit(solution)/shard_map/ppermute | solution.py:380
  9.4 5.6 %collective-permute-start.1 = (bf16[128,512]{1,0:T(8,128)(2,1)S(1)}, bf16[128,512]{1,0:T(8,128)(2,1)S(1)}, u32[]{:S(2)}, u32[]{:S(2)}) collective-permute-start(bf16[128,512]{1,0:T(8,128)(2,1)S(1)} %get-tuple-element.21), channel_id=1, source_target_pairs={{0,2},{1,3},{2,0},{3,1},{4,6},{5,7},{6,4},{7,5},{8,10},{9,11},{10,... | collective-permute-start | bytes 393224 | tf_op jit(solution)/shard_map/ppermute | solution.py:377
  10.9 5.8 %collective-permute-start.2 = (bf16[128,512]{1,0:T(8,128)(2,1)S(1)}, bf16[128,512]{1,0:T(8,128)(2,1)S(1)}, u32[]{:S(2)}, u32[]{:S(2)}) collective-permute-start(bf16[128,512]{1,0:T(8,128)(2,1)S(1)} %get-tuple-element.22), channel_id=1, source_target_pairs={{0,3},{1,2},{2,1},{3,0},{4,7},{5,6},{6,5},{7,4},{8,11},{9,10},{10,... | collective-permute-start | bytes 393224 | tf_op jit(solution)/shard_map/ppermute | solution.py:377
  16.7 1.0 %copy-start.1 = (bf16[128,1024]{1,0:T(8,128)(2,1)S(1)}, bf16[128,1024]{1,0:T(8,128)(2,1)}, u32[]{:S(2)}) copy-start(bf16[128,1024]{1,0:T(8,128)(2,1)} %get-tuple-element.19.refs_2_.refs_1_) | copy-start | bytes 786436
  17.7 0.9 %copy-start.7 = (bf16[128,1024]{1,0:T(8,128)(2,1)S(1)}, bf16[128,1024]{1,0:T(8,128)(2,1)}, u32[]{:S(2)}) copy-start(bf16[128,1024]{1,0:T(8,128)(2,1)} %get-tuple-element.20.refs_0_) | copy-start | bytes 786436
  17.7 1.0 %copy-start.6 = (bf16[128,1024]{1,0:T(8,128)(2,1)S(1)}, bf16[128,1024]{1,0:T(8,128)(2,1)}, u32[]{:S(2)}) copy-start(bf16[128,1024]{1,0:T(8,128)(2,1)} %get-tuple-element.23.refs_0_) | copy-start | bytes 786436
  17.7 13.3 %collective-permute-start.8 = (bf16[256,512]{1,0:T(8,128)(2,1)S(1)}, bf16[256,512]{1,0:T(8,128)(2,1)S(1)}, u32[]{:S(2)}, u32[]{:S(2)}) collective-permute-start(bf16[256,512]{1,0:T(8,128)(2,1)S(1)} %shard_map.59.refs_1_.refs_0_), channel_id=1, source_target_pairs={{0,4},{4,0},{8,12},{12,8},{1,5},{5,1},{9,13},{13,9},{2,6},{6,2},{1... | collective-permute-start | bytes 786440 | tf_op jit(solution)/shard_map/ppermute | solution.py:380
  18.2 15.1 %collective-permute-start.7 = (bf16[256,512]{1,0:T(8,128)(2,1)S(1)}, bf16[256,512]{1,0:T(8,128)(2,1)S(1)}, u32[]{:S(2)}, u32[]{:S(2)}) collective-permute-start(bf16[256,512]{1,0:T(8,128)(2,1)S(1)} %shard_map.59.refs_1_.refs_0_), channel_id=1, source_target_pairs={{0,8},{4,12},{8,0},{12,4},{1,9},{5,13},{9,1},{13,5},{2,10},{6,14},... | collective-permute-start | bytes 786440 | tf_op jit(solution)/shard_map/ppermute | solution.py:380
  18.6 3.5 %copy-start = (bf16[1024,512]{1,0:T(8,128)(2,1)S(1)}, bf16[1024,512]{1,0:T(8,128)(2,1)}, u32[]{:S(2)}) copy-start(bf16[1024,512]{1,0:T(8,128)(2,1)} %ck_ref.11) | copy-start | bytes 3145732
  18.7 1.0 %copy-start.5 = (bf16[128,1024]{1,0:T(8,128)(2,1)S(1)}, bf16[128,1024]{1,0:T(8,128)(2,1)}, u32[]{:S(2)}) copy-start(bf16[128,1024]{1,0:T(8,128)(2,1)} %get-tuple-element.24.refs_0_) | copy-start | bytes 786436
  19.8 15.5 %collective-permute-start.5 = (bf16[128,1024]{1,0:T(8,128)(2,1)S(1)}, bf16[128,1024]{1,0:T(8,128)(2,1)S(1)}, u32[]{:S(2)}, u32[]{:S(2)}) collective-permute-start(bf16[128,1024]{1,0:T(8,128)(2,1)S(1)} %shard_map.62), channel_id=1, source_target_pairs={{0,3},{1,2},{2,1},{3,0},{4,7},{5,6},{6,5},{7,4},{8,11},{9,10},{10,... | collective-permute-start | bytes 786440 | tf_op jit(solution)/shard_map/ppermute | solution.py:377
  21.6 13.7 %collective-permute-start.4 = (bf16[128,1024]{1,0:T(8,128)(2,1)S(1)}, bf16[128,1024]{1,0:T(8,128)(2,1)S(1)}, u32[]{:S(2)}, u32[]{:S(2)}) collective-permute-start(bf16[128,1024]{1,0:T(8,128)(2,1)S(1)} %shard_map.61), channel_id=1, source_target_pairs={{0,2},{1,3},{2,0},{3,1},{4,6},{5,7},{6,4},{7,5},{8,10},{9,11},{10,... | collective-permute-start | bytes 786440 | tf_op jit(solution)/shard_map/ppermute | solution.py:377
  22.1 13.2 %collective-permute-start.3 = (bf16[128,1024]{1,0:T(8,128)(2,1)S(1)}, bf16[128,1024]{1,0:T(8,128)(2,1)S(1)}, u32[]{:S(2)}, u32[]{:S(2)}) collective-permute-start(bf16[128,1024]{1,0:T(8,128)(2,1)S(1)} %shard_map.60), channel_id=1, source_target_pairs={{0,1},{1,0},{2,3},{3,2},{4,5},{5,4},{6,7},{7,6},{8,9},{9,8},{10,11... | collective-permute-start | bytes 786440 | tf_op jit(solution)/shard_map/ppermute | solution.py:377
  33.4 9.3 %collective-permute-start.15 = (bf16[256,512]{1,0:T(8,128)(2,1)S(1)}, bf16[256,512]{1,0:T(8,128)(2,1)S(1)}, u32[]{:S(2)}, u32[]{:S(2)}) collective-permute-start(bf16[256,512]{1,0:T(8,128)(2,1)S(1)} %shard_map.73), channel_id=1, source_target_pairs={{0,4},{4,0},{8,12},{12,8},{1,5},{5,1},{9,13},{13,9},{2,6},{6,2},{1... | collective-permute-start | bytes 786440 | tf_op jit(solution)/shard_map/ppermute | solution.py:380
  35.4 12.9 %collective-permute-start.9 = (bf16[256,512]{1,0:T(8,128)(2,1)S(1)}, bf16[256,512]{1,0:T(8,128)(2,1)S(1)}, u32[]{:S(2)}, u32[]{:S(2)}) collective-permute-start(bf16[256,512]{1,0:T(8,128)(2,1)S(1)} %shard_map.66), channel_id=1, source_target_pairs={{0,4},{4,0},{8,12},{12,8},{1,5},{5,1},{9,13},{13,9},{2,6},{6,2},{1... | collective-permute-start | bytes 786440 | tf_op jit(solution)/shard_map/ppermute | solution.py:380
  44.5 9.6 %collective-permute-start.16 = (s16[528,256]{1,0:T(8,128)(2,1)S(1)}, s16[528,256]{1,0:T(8,128)(2,1)S(1)}, u32[]{:S(2)}, u32[]{:S(2)}) collective-permute-start(s16[528,256]{1,0:T(8,128)(2,1)S(1)} %shard_map.74), channel_id=1, source_target_pairs={{0,4},{4,0},{8,12},{12,8},{1,5},{5,1},{9,13},{13,9},{2,6},{6,2},{1... | collective-permute-start | bytes 811016 | tf_op jit(solution)/shard_map/ppermute | solution.py:380
  50.1 15.5 %collective-permute-start.10 = (s16[528,256]{1,0:T(8,128)(2,1)S(1)}, s16[528,256]{1,0:T(8,128)(2,1)S(1)}, u32[]{:S(2)}, u32[]{:S(2)}) collective-permute-start(s16[528,256]{1,0:T(8,128)(2,1)S(1)} %shard_map.67), channel_id=1, source_target_pairs={{0,4},{4,0},{8,12},{12,8},{1,5},{5,1},{9,13},{13,9},{2,6},{6,2},{1... | collective-permute-start | bytes 811016 | tf_op jit(solution)/shard_map/ppermute | solution.py:380
  54.3 22.9 %collective-permute-start.18 = (s16[528,256]{1,0:T(8,128)(2,1)S(1)}, s16[528,256]{1,0:T(8,128)(2,1)S(1)}, u32[]{:S(2)}, u32[]{:S(2)}) collective-permute-start(s16[528,256]{1,0:T(8,128)(2,1)S(1)} %shard_map.77), channel_id=1, source_target_pairs={{0,4},{4,0},{8,12},{12,8},{1,5},{5,1},{9,13},{13,9},{2,6},{6,2},{1... | collective-permute-start | bytes 811016 | tf_op jit(solution)/shard_map/ppermute | solution.py:380
  54.4 22.8 %collective-permute-start.17 = (s16[528,256]{1,0:T(8,128)(2,1)S(1)}, s16[528,256]{1,0:T(8,128)(2,1)S(1)}, u32[]{:S(2)}, u32[]{:S(2)}) collective-permute-start(s16[528,256]{1,0:T(8,128)(2,1)S(1)} %shard_map.75.refs_1_), channel_id=1, source_target_pairs={{0,8},{4,12},{8,0},{12,4},{1,9},{5,13},{9,1},{13,5},{2,10},{6,14},... | collective-permute-start | bytes 811016 | tf_op jit(solution)/shard_map/ppermute | solution.py:380
  65.9 1.2 %copy-start.2 = (bf16[128,1024]{1,0:T(8,128)(2,1)S(1)}, bf16[128,1024]{1,0:T(8,128)(2,1)}, u32[]{:S(2)}) copy-start(bf16[128,1024]{1,0:T(8,128)(2,1)} %get-tuple-element.19.refs_2_.refs_1_) | copy-start | bytes 786436
  65.9 1.2 %copy-start.9 = (s32[4]{0:T(128)S(1)}, s32[4]{0:T(128)}, u32[]{:S(2)}) copy-start(s32[4]{0:T(128)} %copy-done.8) | copy-start | bytes 52
  66.0 15.6 %collective-permute-start.13 = (s16[528,256]{1,0:T(8,128)(2,1)S(1)}, s16[528,256]{1,0:T(8,128)(2,1)S(1)}, u32[]{:S(2)}, u32[]{:S(2)}) collective-permute-start(s16[528,256]{1,0:T(8,128)(2,1)S(1)} %shard_map.70), channel_id=1, source_target_pairs={{0,4},{4,0},{8,12},{12,8},{1,5},{5,1},{9,13},{13,9},{2,6},{6,2},{1... | collective-permute-start | bytes 811016 | tf_op jit(solution)/shard_map/ppermute | solution.py:380
  66.0 15.5 %collective-permute-start.11 = (s16[528,256]{1,0:T(8,128)(2,1)S(1)}, s16[528,256]{1,0:T(8,128)(2,1)S(1)}, u32[]{:S(2)}, u32[]{:S(2)}) collective-permute-start(s16[528,256]{1,0:T(8,128)(2,1)S(1)} %shard_map.68.refs_1_), channel_id=1, source_target_pairs={{0,8},{4,12},{8,0},{12,4},{1,9},{5,13},{9,1},{13,5},{2,10},{6,14},... | collective-permute-start | bytes 811016 | tf_op jit(solution)/shard_map/ppermute | solution.py:380
  77.6 6.1 %collective-permute-start.19 = (bf16[128,512]{1,0:T(8,128)(2,1)S(1)}, bf16[128,512]{1,0:T(8,128)(2,1)S(1)}, u32[]{:S(2)}, u32[]{:S(2)}) collective-permute-start(bf16[128,512]{1,0:T(8,128)(2,1)S(1)} %get-tuple-element.27), channel_id=1, source_target_pairs={{0,2},{1,3},{2,0},{3,1},{4,6},{5,7},{6,4},{7,5},{8,10},{9,11},{10,... | collective-permute-start | bytes 393224 | tf_op jit(solution)/shard_map/ppermute | solution.py:377
  78.5 5.8 %collective-permute-start.20 = (bf16[128,512]{1,0:T(8,128)(2,1)S(1)}, bf16[128,512]{1,0:T(8,128)(2,1)S(1)}, u32[]{:S(2)}, u32[]{:S(2)}) collective-permute-start(bf16[128,512]{1,0:T(8,128)(2,1)S(1)} %get-tuple-element.28), channel_id=1, source_target_pairs={{0,3},{1,2},{2,1},{3,0},{4,7},{5,6},{6,5},{7,4},{8,11},{9,10},{10,... | collective-permute-start | bytes 393224 | tf_op jit(solution)/shard_map/ppermute | solution.py:377
  81.9 2.4 %collective-permute-start.14 = (bf16[128,512]{1,0:T(8,128)(2,1)S(1)}, bf16[128,512]{1,0:T(8,128)(2,1)S(1)}, u32[]{:S(2)}, u32[]{:S(2)}) collective-permute-start(bf16[128,512]{1,0:T(8,128)(2,1)S(1)} %get-tuple-element.26), channel_id=1, source_target_pairs={{0,1},{1,0},{2,3},{3,2},{4,5},{5,4},{6,7},{7,6},{8,9},{9,8},{10,11... | collective-permute-start | bytes 393224 | tf_op jit(solution)/shard_map/ppermute | solution.py:377

commit v2 on v0

--- a/solution.py
+++ b/solution.py
@@ -188,7 +188,8 @@
         most = jnp.maximum(jnp.max(jnp.abs(numer), axis=0, keepdims=True), LEAST)
         code = jnp.round(numer * (UNIT / most))
         out_ref[h * HD : (h + 1) * HD, :] = code.astype(jnp.int32).astype(jnp.int16)
-        for j, value in enumerate((top + jnp.log2(denom), jnp.log2(most / (UNIT * denom)))):
+        weight = jnp.log2(denom)
+        for j, value in enumerate((top + weight, jnp.log2(most) - math.log2(UNIT) - weight)):
             whole = jnp.floor(value)
             stats = jnp.where(at == 4 * h + 2 * j, whole, stats)
             stats = jnp.where(at == 4 * h + 2 * j + 1, jnp.round((value - whole) * UNIT), stats)

time: 84.7 us -> 84.7 us (level)
  no operation moved by 1% of the time
where the time goes in v2:
time: 84.7 us; the launch traced here: 84.5 us
  waiting for transfers between devices  36.7 us (43%)
  Pallas kernels  25.4 us (30%)
  starting transfers between devices  19.7 us (23%)
  local copies, waits for them, and re-layouts  2.4 us (3%)
    ppermute x12, waiting for transfers between devices, along(): return lax.ppermute(x, 'seq', [(i, i ^ bit) for i in range(seq_count)])  26.3 us
    pallas_call x21, Pallas kernels, call(): pl.pallas_call(kernel, out_shape=outs, in_specs=[pl.BlockSpec(memory_spac...  22.3 us
    ppermute x12, starting transfers between devices, along(): return lax.ppermute(x, 'seq', [(i, i ^ bit) for i in range(seq_count)])  13.7 us
    ppermute x9, waiting for transfers between devices, swap(): lax.ppermute(x, ('heads', 'sub'), [(i, i ^ d) for i in range(shares)])  10.3 us
    ppermute x9, starting transfers between devices, swap(): lax.ppermute(x, ('heads', 'sub'), [(i, i ^ d) for i in range(shares)])  6 us
    pallas_call x1, Pallas kernels, move(): pl.pallas_call(without_unread, out_shape=outs, in_specs=[pl.BlockSpec(mem...  3.14 us
    unnamed x21, local copies, waits for them, and re-layouts  2.4 us
  transfers between devices with their start and end apart: 21, of which 13 were waited for; matrix products, arithmetic and copies ran while one was open for 2% of the time, Pallas kernels for 28%

profile of v2, /device:TPU:0, one launch (start us, length us, event | category | flops | bytes accessed | tf_op | source)
XLA Modules:
  0.0 84.5 jit_solution(4297896657052662946)
XLA Ops:
  0.0 0.1 pad_add_fusion.order_ref.refs_0_
  0.1 1.0 %copy-done.4 = bf16[128,2048]{1,0:T(8,128)(2,1)S(1)} copy-done((bf16[128,2048]{1,0:T(8,128)(2,1)S(1)}, bf16[128,2048]{1,0:T(8,128)(2,1)}, u32[]{:S(2)}) %copy-start.4) | copy-done | bytes 524312
  1.1 0.6 shard_map.55
  1.7 0.5 collective-permute-start
  2.2 1.0 %collective-permute-done.refs_1_ = bf16[128,512]{1,0:T(8,128)(2,1)S(1)} collective-permute-done((bf16[128,512]{1,0:T(8,128)(2,1)S(1)}, bf16[128,512]{1,0:T(8,128)(2,1)S(1)}, u32[]{:S(2)}, u32[]{:S(2)}) %collective-permute-start) | collective-permute-done | bytes 131104 | tf_op jit(solution)/shard_map/ppermute | solution.py:378
  3.2 3.0 %collective-permute-start.12 = (bf16[256,512]{1,0:T(8,128)(2,1)S(1)}, bf16[256,512]{1,0:T(8,128)(2,1)}, u32[]{:S(2)}, u32[]{:S(2)}) collective-permute-start(bf16[256,512]{1,0:T(8,128)(2,1)S(1)} %shard_map.56.refs_0_), channel_id=1, source_target_pairs={{0,4},{4,0},{8,12},{12,8},{1,5},{5,1},{9,13},{13,9},{2,6},{6,2},{1... | collective-permute-start | bytes 786440 | tf_op jit(solution)/shard_map/ppermute | solution.py:381
  6.2 2.6 %collective-permute-start.6 = (bf16[256,512]{1,0:T(8,128)(2,1)S(1)}, bf16[256,512]{1,0:T(8,128)(2,1)S(1)}, u32[]{:S(2)}, u32[]{:S(2)}) collective-permute-start(bf16[256,512]{1,0:T(8,128)(2,1)S(1)} %shard_map.56.refs_0_), channel_id=1, source_target_pairs={{0,8},{4,12},{8,0},{12,4},{1,9},{5,13},{9,1},{13,5},{2,10},{6,14},... | collective-permute-start | bytes 786440 | tf_op jit(solution)/shard_map/ppermute | solution.py:381
  8.8 0.0 copy-done.7
  8.8 0.6 shard_map.57
  9.4 1.6 %collective-permute-start.1 = (bf16[128,512]{1,0:T(8,128)(2,1)S(1)}, bf16[128,512]{1,0:T(8,128)(2,1)S(1)}, u32[]{:S(2)}, u32[]{:S(2)}) collective-permute-start(bf16[128,512]{1,0:T(8,128)(2,1)S(1)} %get-tuple-element.19), channel_id=1, source_target_pairs={{0,2},{1,3},{2,0},{3,1},{4,6},{5,7},{6,4},{7,5},{8,10},{9,11},{10,... | collective-permute-start | bytes 393224 | tf_op jit(solution)/shard_map/ppermute | solution.py:378
  10.9 0.0 collective-permute-start.2
  10.9 4.0 %collective-permute-done.1.refs_0_ = bf16[128,512]{1,0:T(8,128)(2,1)S(1)} collective-permute-done((bf16[128,512]{1,0:T(8,128)(2,1)S(1)}, bf16[128,512]{1,0:T(8,128)(2,1)S(1)}, u32[]{:S(2)}, u32[]{:S(2)}) %collective-permute-start.1) | collective-permute-done | bytes 131104 | tf_op jit(solution)/shard_map/ppermute | solution.py:378
  15.0 1.8 %collective-permute-done.2.refs_1_ = bf16[128,512]{1,0:T(8,128)(2,1)S(1)} collective-permute-done((bf16[128,512]{1,0:T(8,128)(2,1)S(1)}, bf16[128,512]{1,0:T(8,128)(2,1)S(1)}, u32[]{:S(2)}, u32[]{:S(2)}) %collective-permute-start.2) | collective-permute-done | bytes 131104 | tf_op jit(solution)/shard_map/ppermute | solution.py:378
  16.7 0.0 copy-start.2
  16.8 0.4 collective-permute-start.7
  17.2 1.3 %copy.6 = bf16[1024,512]{0,1:T(8,128)(2,1)} copy(bf16[1024,512]{1,0:T(8,128)(2,1)S(1)} %copy-done.9) | data formatting | bytes 2097152 | tf_op args[4]
  18.5 0.5 collective-permute-start.8
  19.0 3.1 %shard_map.59 = (bf16[128,1024]{1,0:T(8,128)(2,1)}, bf16[128,1024]{1,0:T(8,128)(2,1)}, bf16[128,1024]{1,0:T(8,128)(2,1)}, bf16[128,1024]{1,0:T(8,128)(2,1)}) custom-call(s32[4]{0:T(128)} %copy-done.7, bf16[128,2048]{1,0:T(8,128)(2,1)} %refs_1_.1, bf16[128,2048]{1,0:T(8,128)(2,1)} %refs_2_.1, bf16[256,512]{1,0:T(8,128)(2,1)} %copy-done.2, ...), custom_call_target="tpu_custom_call" | custom-call | bytes 1048576 | tf_op jit(solution)/shard_map/pallas_call | solution.py:335
  22.2 0.1 collective-permute-start.3
  22.3 0.0 collective-permute-done.12.q_ref
  22.3 1.5 %collective-permute-start.4 = (bf16[128,1024]{1,0:T(8,128)(2,1)}, bf16[128,1024]{1,0:T(8,128)(2,1)S(1)}, u32[]{:S(2)}, u32[]{:S(2)}) collective-permute-start(bf16[128,1024]{1,0:T(8,128)(2,1)} %get-tuple-element.23), channel_id=1, source_target_pairs={{0,2},{1,3},{2,0},{3,1},{4,6},{5,7},{6,4},{7,5},{8,10},{9,11},{10,... | collective-permute-start | bytes 786440 | tf_op jit(solution)/shard_map/ppermute | solution.py:378
  23.8 2.3 %collective-permute-done.6.q_ref.refs_0_ = bf16[256,512]{1,0:T(8,128)(2,1)S(1)} collective-permute-done((bf16[256,512]{1,0:T(8,128)(2,1)S(1)}, bf16[256,512]{1,0:T(8,128)(2,1)S(1)}, u32[]{:S(2)}, u32[]{:S(2)}) %collective-permute-start.6) | collective-permute-done | bytes 262176 | tf_op jit(solution)/shard_map/ppermute | solution.py:381
  26.2 0.0 collective-permute-start.5
  26.2 2.8 %shard_map.66.refs_0_.refs_2_ = s16[528,256]{1,0:T(8,128)(2,1)S(1)} custom-call(bf16[256,512]{1,0:T(8,128)(2,1)} %collective-permute-done.12.q_ref, bf16[1024,512]{1,0:T(8,128)(2,1)S(1)} %copy-done.1, bf16[512,1024]{1,0:T(8,128)(2,1)S(1)} %bitcast.6), custom_call_target="tpu_custom_call" | custom-call | flops 536870912 | bytes 2629632 | tf_op jit(solution)/shard_map/pallas_call | solution.py:350
  28.9 1.8 %shard_map.61.refs_0_.refs_1_ = s16[528,256]{1,0:T(8,128)(2,1)S(1)} custom-call(bf16[256,512]{1,0:T(8,128)(2,1)S(1)} %collective-permute-done.6.q_ref.refs_0_, bf16[1024,512]{1,0:T(8,128)(2,1)S(1)} %copy-done.1, bf16[512,1024]{1,0:T(8,128)(2,1)S(1)} %bitcast.7), custom_call_target="tpu_custom_call" | custom-call | flops 536870912 | bytes 2629632 | tf_op jit(solution)/shard_map/pallas_call | solution.py:350
  30.8 1.4 %collective-permute-done.7.q_ref.refs_0_ = bf16[256,512]{1,0:T(8,128)(2,1)S(1)} collective-permute-done((bf16[256,512]{1,0:T(8,128)(2,1)S(1)}, bf16[256,512]{1,0:T(8,128)(2,1)S(1)}, u32[]{:S(2)}, u32[]{:S(2)}) %collective-permute-start.7) | collective-permute-done | bytes 262176 | tf_op jit(solution)/shard_map/ppermute | solution.py:381
  32.2 0.1 collective-permute-start.15
  32.2 1.8 %shard_map.62.refs_1_.refs_0_ = s16[528,256]{1,0:T(8,128)(2,1)S(1)} custom-call(bf16[256,512]{1,0:T(8,128)(2,1)S(1)} %collective-permute-done.7.q_ref.refs_0_, bf16[1024,512]{1,0:T(8,128)(2,1)S(1)} %copy-done.1, bf16[512,1024]{1,0:T(8,128)(2,1)S(1)} %bitcast.8), custom_call_target="tpu_custom_call" | custom-call | flops 536870912 | bytes 2629632 | tf_op jit(solution)/shard_map/pallas_call | solution.py:350
  34.1 0.0 collective-permute-done.8.refs_2_.q_ref
  34.1 0.0 collective-permute-done.3.refs_2_.refs_3_
  34.1 0.0 collective-permute-done.4.refs_3_.refs_4_
  34.1 2.2 %collective-permute-done.5.refs_4_.refs_5_ = bf16[128,1024]{1,0:T(8,128)(2,1)S(1)} collective-permute-done((bf16[128,1024]{1,0:T(8,128)(2,1)}, bf16[128,1024]{1,0:T(8,128)(2,1)S(1)}, u32[]{:S(2)}, u32[]{:S(2)}) %collective-permute-start.5) | collective-permute-done | bytes 262176 | tf_op jit(solution)/shard_map/ppermute | solution.py:378
  36.3 1.5 %collective-permute-start.9 = (bf16[256,512]{1,0:T(8,128)(2,1)S(1)}, bf16[256,512]{1,0:T(8,128)(2,1)S(1)}, u32[]{:S(2)}, u32[]{:S(2)}) collective-permute-start(bf16[256,512]{1,0:T(8,128)(2,1)S(1)} %shard_map.63), channel_id=1, source_target_pairs={{0,4},{4,0},{8,12},{12,8},{1,5},{5,1},{9,13},{13,9},{2,6},{6,2},{1... | collective-permute-start | bytes 786440 | tf_op jit(solution)/shard_map/ppermute | solution.py:381
  37.8 3.5 %collective-permute-done.15.q_ref = bf16[256,512]{1,0:T(8,128)(2,1)S(1)} collective-permute-done((bf16[256,512]{1,0:T(8,128)(2,1)S(1)}, bf16[256,512]{1,0:T(8,128)(2,1)S(1)}, u32[]{:S(2)}, u32[]{:S(2)}) %collective-permute-start.15) | collective-permute-done | bytes 262176 | tf_op jit(solution)/shard_map/ppermute | solution.py:381
  41.3 1.8 %shard_map.71 = s16[528,256]{1,0:T(8,128)(2,1)S(1)} custom-call(bf16[256,512]{1,0:T(8,128)(2,1)S(1)} %collective-permute-done.15.q_ref, bf16[1024,512]{1,0:T(8,128)(2,1)S(1)} %copy-done.1, bf16[512,1024]{1,0:T(8,128)(2,1)S(1)} %bitcast.9), custom_call_target="tpu_custom_call" | custom-call | flops 536870912 | bytes 2629632 | tf_op jit(solution)/shard_map/pallas_call | solution.py:350
  43.1 0.1 collective-permute-start.16
  43.2 3.7 %collective-permute-done.9.q_ref = bf16[256,512]{1,0:T(8,128)(2,1)S(1)} collective-permute-done((bf16[256,512]{1,0:T(8,128)(2,1)S(1)}, bf16[256,512]{1,0:T(8,128)(2,1)S(1)}, u32[]{:S(2)}, u32[]{:S(2)}) %collective-permute-start.9) | collective-permute-done | bytes 262176 | tf_op jit(solution)/shard_map/ppermute | solution.py:381
  46.9 1.8 %shard_map.64 = s16[528,256]{1,0:T(8,128)(2,1)S(1)} custom-call(bf16[256,512]{1,0:T(8,128)(2,1)S(1)} %collective-permute-done.9.q_ref, bf16[1024,512]{1,0:T(8,128)(2,1)S(1)} %copy-done.1, bf16[512,1024]{1,0:T(8,128)(2,1)S(1)} %bitcast.10), custom_call_target="tpu_custom_call" | custom-call | flops 536870912 | bytes 2629632 | tf_op jit(solution)/shard_map/pallas_call | solution.py:350
  48.8 0.2 collective-permute-start.10
  48.9 1.8 %shard_map.73.refs_0_ = s16[528,256]{1,0:T(8,128)(2,1)S(1)} custom-call(bf16[256,512]{1,0:T(8,128)(2,1)S(1)} %collective-permute-done.8.refs_2_.q_ref, bf16[1024,512]{1,0:T(8,128)(2,1)S(1)} %copy-done.1, bf16[512,1024]{1,0:T(8,128)(2,1)S(1)} %bitcast.11), custom_call_target="tpu_custom_call" | custom-call | flops 536870912 | bytes 2629632 | tf_op jit(solution)/shard_map/pallas_call | solution.py:350
  50.8 2.0 %collective-permute-done.16.refs_1_ = s16[528,256]{1,0:T(8,128)(2,1)S(1)} collective-permute-done((s16[528,256]{1,0:T(8,128)(2,1)S(1)}, s16[528,256]{1,0:T(8,128)(2,1)S(1)}, u32[]{:S(2)}, u32[]{:S(2)}) %collective-permute-start.16) | collective-permute-done | bytes 270368 | tf_op jit(solution)/shard_map/ppermute | solution.py:381
  52.7 0.2 shard_map.72.refs_1_
  53.0 0.2 collective-permute-start.18
  53.2 2.6 %collective-permute-start.17 = (s16[528,256]{1,0:T(8,128)(2,1)S(1)}, s16[528,256]{1,0:T(8,128)(2,1)S(1)}, u32[]{:S(2)}, u32[]{:S(2)}) collective-permute-start(s16[528,256]{1,0:T(8,128)(2,1)S(1)} %shard_map.72.refs_1_), channel_id=1, source_target_pairs={{0,8},{4,12},{8,0},{12,4},{1,9},{5,13},{9,1},{13,5},{2,10},{6,14},... | collective-permute-start | bytes 811016 | tf_op jit(solution)/shard_map/ppermute | solution.py:381
  55.7 8.6 %collective-permute-done.10.refs_1_ = s16[528,256]{1,0:T(8,128)(2,1)S(1)} collective-permute-done((s16[528,256]{1,0:T(8,128)(2,1)S(1)}, s16[528,256]{1,0:T(8,128)(2,1)S(1)}, u32[]{:S(2)}, u32[]{:S(2)}) %collective-permute-start.10) | collective-permute-done | bytes 270368 | tf_op jit(solution)/shard_map/ppermute | solution.py:381
  64.3 0.2 shard_map.65.refs_1_
  64.6 0.0 copy-start.3
  64.6 0.1 collective-permute-start.13
  64.7 2.7 %collective-permute-start.11 = (s16[528,256]{1,0:T(8,128)(2,1)S(1)}, s16[528,256]{1,0:T(8,128)(2,1)S(1)}, u32[]{:S(2)}, u32[]{:S(2)}) collective-permute-start(s16[528,256]{1,0:T(8,128)(2,1)S(1)} %shard_map.65.refs_1_), channel_id=1, source_target_pairs={{0,8},{4,12},{8,0},{12,4},{1,9},{5,13},{9,1},{13,5},{2,10},{6,14},... | collective-permute-start | bytes 811016 | tf_op jit(solution)/shard_map/ppermute | solution.py:381
  67.4 3.4 %shard_map.69.refs_0_ = s16[528,256]{1,0:T(8,128)(2,1)S(1)} custom-call(s32[4]{0:T(128)S(1)} %copy-done.8, bf16[256,512]{1,0:T(8,128)(2,1)S(1)} %copy-done.3, bf16[128,1024]{1,0:T(8,128)(2,1)S(1)} %copy-done.6, bf16[128,1024]{1,0:T(8,128)(2,1)S(1)} %collective-permute-done.3.refs_2_.refs_3_, bf16[128,1024]{1,0:T(8,128)(2,1)S(1)} %collective-permute-done.4.refs_3_.refs_4_, ...), custom_call_target="tpu_custom_call" | custom-call | flops 805306368 | bytes 3678208 | tf_op jit(solution)/shard_map/pallas_call | solution.py:350
  70.8 3.3 %shard_map.60.refs_0_ = s16[528,256]{1,0:T(8,128)(2,1)S(1)} custom-call(s32[4]{0:T(128)S(1)} %copy-done.8, bf16[256,512]{1,0:T(8,128)(2,1)S(1)} %shard_map.56.refs_0_, bf16[128,1024]{1,0:T(8,128)(2,1)S(1)} %copy-done.6, bf16[128,1024]{1,0:T(8,128)(2,1)S(1)} %collective-permute-done.3.refs_2_.refs_3_, ...), custom_call_target="tpu_custom_call" | custom-call | flops 805306368 | bytes 3678208 | tf_op jit(solution)/shard_map/pallas_call | solution.py:350
  74.1 0.0 collective-permute-done.18.refs_2_
  74.1 0.0 collective-permute-done.17.refs_1_
  74.1 0.3 shard_map.75
  74.4 2.2 %collective-permute-start.19 = (bf16[128,512]{1,0:T(8,128)(2,1)S(1)}, bf16[128,512]{1,0:T(8,128)(2,1)S(1)}, u32[]{:S(2)}, u32[]{:S(2)}) collective-permute-start(bf16[128,512]{1,0:T(8,128)(2,1)S(1)} %get-tuple-element.27), channel_id=1, source_target_pairs={{0,2},{1,3},{2,0},{3,1},{4,6},{5,7},{6,4},{7,5},{8,10},{9,11},{10,... | collective-permute-start | bytes 393224 | tf_op jit(solution)/shard_map/ppermute | solution.py:378
  76.6 0.0 collective-permute-start.20
  76.6 4.9 %collective-permute-done.13.refs_2_ = s16[528,256]{1,0:T(8,128)(2,1)S(1)} collective-permute-done((s16[528,256]{1,0:T(8,128)(2,1)S(1)}, s16[528,256]{1,0:T(8,128)(2,1)S(1)}, u32[]{:S(2)}, u32[]{:S(2)}) %collective-permute-start.13) | collective-permute-done | bytes 270368 | tf_op jit(solution)/shard_map/ppermute | solution.py:381
  81.4 0.0 collective-permute-done.11.refs_1_
  81.4 0.3 shard_map.68
  81.7 0.1 collective-permute-start.14
  81.8 0.0 collective-permute-done.19.refs_2_
  81.8 1.2 %collective-permute-done.20.refs_3_ = bf16[128,512]{1,0:T(8,128)(2,1)S(1)} collective-permute-done((bf16[128,512]{1,0:T(8,128)(2,1)S(1)}, bf16[128,512]{1,0:T(8,128)(2,1)S(1)}, u32[]{:S(2)}, u32[]{:S(2)}) %collective-permute-start.20) | collective-permute-done | bytes 131104 | tf_op jit(solution)/shard_map/ppermute | solution.py:378
  83.1 0.1 collective-permute-done.14.refs_1_
  83.2 1.4 %shard_map.76 = bf16[128,2048]{1,0:T(8,128)(2,1)} custom-call(s32[4]{0:T(128)S(1)} %copy-done.8, bf16[128,512]{1,0:T(8,128)(2,1)S(1)} %get-tuple-element.25.refs_0_, bf16[128,512]{1,0:T(8,128)(2,1)S(1)} %collective-permute-done.14.refs_1_, bf16[128,512]{1,0:T(8,128)(2,1)S(1)} %collective-permute-done.19.refs_2_, ...), custom_call_target="tpu_custom_call" | custom-call | bytes 1048576 | tf_op jit(solution)/shard_map/pallas_call | solution.py:350
  (22 shorter events, 0.1 us)
Async XLA Ops:
  0.1 1.0 %copy-start.4 = (bf16[128,2048]{1,0:T(8,128)(2,1)S(1)}, bf16[128,2048]{1,0:T(8,128)(2,1)}, u32[]{:S(2)}) copy-start(bf16[128,2048]{1,0:T(8,128)(2,1)} %ref.3) | copy-start | bytes 1572868
  1.1 7.7 %copy-start.7 = (s32[4]{0:T(128)}, s32[4]{0:T(128)S(1)}, u32[]{:S(2)}) copy-start(s32[4]{0:T(128)S(1)} %pad_add_fusion.order_ref.refs_0_) | copy-start | bytes 52
  1.1 7.7 %copy-start.5 = (bf16[128,2048]{1,0:T(8,128)(2,1)S(1)}, bf16[128,2048]{1,0:T(8,128)(2,1)}, u32[]{:S(2)}) copy-start(bf16[128,2048]{1,0:T(8,128)(2,1)} %ref.3) | copy-start | bytes 1572868
  1.1 16.0 %copy-start.9 = (bf16[1024,512]{1,0:T(8,128)(2,1)S(1)}, bf16[1024,512]{1,0:T(8,128)(2,1)}, u32[]{:S(2)}) copy-start(bf16[1024,512]{1,0:T(8,128)(2,1)} %param.10) | copy-start | bytes 3145732
  1.7 1.5 %collective-permute-start = (bf16[128,512]{1,0:T(8,128)(2,1)S(1)}, bf16[128,512]{1,0:T(8,128)(2,1)S(1)}, u32[]{:S(2)}, u32[]{:S(2)}) collective-permute-start(bf16[128,512]{1,0:T(8,128)(2,1)S(1)} %get-tuple-element.18), channel_id=1, source_target_pairs={{0,1},{1,0},{2,3},{3,2},{4,5},{5,4},{6,7},{7,6},{8,9},{9,8},{10,11... | collective-permute-start | bytes 393224 | tf_op jit(solution)/shard_map/ppermute | solution.py:378
  3.2 19.1 %collective-permute-start.12 = (bf16[256,512]{1,0:T(8,128)(2,1)S(1)}, bf16[256,512]{1,0:T(8,128)(2,1)}, u32[]{:S(2)}, u32[]{:S(2)}) collective-permute-start(bf16[256,512]{1,0:T(8,128)(2,1)S(1)} %shard_map.56.refs_0_), channel_id=1, source_target_pairs={{0,4},{4,0},{8,12},{12,8},{1,5},{5,1},{9,13},{13,9},{2,6},{6,2},{1... | collective-permute-start | bytes 786440 | tf_op jit(solution)/shard_map/ppermute | solution.py:381
  6.2 19.9 %collective-permute-start.6 = (bf16[256,512]{1,0:T(8,128)(2,1)S(1)}, bf16[256,512]{1,0:T(8,128)(2,1)S(1)}, u32[]{:S(2)}, u32[]{:S(2)}) collective-permute-start(bf16[256,512]{1,0:T(8,128)(2,1)S(1)} %shard_map.56.refs_0_), channel_id=1, source_target_pairs={{0,8},{4,12},{8,0},{12,4},{1,9},{5,13},{9,1},{13,5},{2,10},{6,14},... | collective-permute-start | bytes 786440 | tf_op jit(solution)/shard_map/ppermute | solution.py:381
  9.4 5.6 %collective-permute-start.1 = (bf16[128,512]{1,0:T(8,128)(2,1)S(1)}, bf16[128,512]{1,0:T(8,128)(2,1)S(1)}, u32[]{:S(2)}, u32[]{:S(2)}) collective-permute-start(bf16[128,512]{1,0:T(8,128)(2,1)S(1)} %get-tuple-element.19), channel_id=1, source_target_pairs={{0,2},{1,3},{2,0},{3,1},{4,6},{5,7},{6,4},{7,5},{8,10},{9,11},{10,... | collective-permute-start | bytes 393224 | tf_op jit(solution)/shard_map/ppermute | solution.py:378
  10.9 5.8 %collective-permute-start.2 = (bf16[128,512]{1,0:T(8,128)(2,1)S(1)}, bf16[128,512]{1,0:T(8,128)(2,1)S(1)}, u32[]{:S(2)}, u32[]{:S(2)}) collective-permute-start(bf16[128,512]{1,0:T(8,128)(2,1)S(1)} %get-tuple-element.20), channel_id=1, source_target_pairs={{0,3},{1,2},{2,1},{3,0},{4,7},{5,6},{6,5},{7,4},{8,11},{9,10},{10,... | collective-permute-start | bytes 393224 | tf_op jit(solution)/shard_map/ppermute | solution.py:378
  16.7 1.7 %copy-start.2 = (bf16[256,512]{1,0:T(8,128)(2,1)}, bf16[256,512]{1,0:T(8,128)(2,1)S(1)}, u32[]{:S(2)}) copy-start(bf16[256,512]{1,0:T(8,128)(2,1)S(1)} %shard_map.58.refs_3_.refs_0_) | copy-start | bytes 786436
  16.8 15.4 %collective-permute-start.7 = (bf16[256,512]{1,0:T(8,128)(2,1)S(1)}, bf16[256,512]{1,0:T(8,128)(2,1)S(1)}, u32[]{:S(2)}, u32[]{:S(2)}) collective-permute-start(bf16[256,512]{1,0:T(8,128)(2,1)S(1)} %shard_map.58.refs_3_.refs_0_), channel_id=1, source_target_pairs={{0,8},{4,12},{8,0},{12,4},{1,9},{5,13},{9,1},{13,5},{2,10},{6,14},... | collective-permute-start | bytes 786440 | tf_op jit(solution)/shard_map/ppermute | solution.py:381
  18.5 15.6 %collective-permute-start.8 = (bf16[256,512]{1,0:T(8,128)(2,1)S(1)}, bf16[256,512]{1,0:T(8,128)(2,1)S(1)}, u32[]{:S(2)}, u32[]{:S(2)}) collective-permute-start(bf16[256,512]{1,0:T(8,128)(2,1)S(1)} %shard_map.58.refs_3_.refs_0_), channel_id=1, source_target_pairs={{0,4},{4,0},{8,12},{12,8},{1,5},{5,1},{9,13},{13,9},{2,6},{6,2},{1... | collective-permute-start | bytes 786440 | tf_op jit(solution)/shard_map/ppermute | solution.py:381
  19.0 7.2 %copy-start = (bf16[1024,512]{0,1:T(8,128)(2,1)S(1)}, bf16[1024,512]{0,1:T(8,128)(2,1)}, u32[]{:S(2)}) copy-start(bf16[1024,512]{0,1:T(8,128)(2,1)} %copy.6) | copy-start | bytes 3145732
  19.0 7.2 %copy-start.1 = (bf16[1024,512]{1,0:T(8,128)(2,1)S(1)}, bf16[1024,512]{1,0:T(8,128)(2,1)}, u32[]{:S(2)}) copy-start(bf16[1024,512]{1,0:T(8,128)(2,1)} %ck_ref.11) | copy-start | bytes 3145732
  22.2 11.9 %collective-permute-start.3 = (bf16[128,1024]{1,0:T(8,128)(2,1)}, bf16[128,1024]{1,0:T(8,128)(2,1)S(1)}, u32[]{:S(2)}, u32[]{:S(2)}) collective-permute-start(bf16[128,1024]{1,0:T(8,128)(2,1)} %get-tuple-element.22), channel_id=1, source_target_pairs={{0,1},{1,0},{2,3},{3,2},{4,5},{5,4},{6,7},{7,6},{8,9},{9,8},{10,11... | collective-permute-start | bytes 786440 | tf_op jit(solution)/shard_map/ppermute | solution.py:378
  22.3 11.8 %collective-permute-start.4 = (bf16[128,1024]{1,0:T(8,128)(2,1)}, bf16[128,1024]{1,0:T(8,128)(2,1)S(1)}, u32[]{:S(2)}, u32[]{:S(2)}) collective-permute-start(bf16[128,1024]{1,0:T(8,128)(2,1)} %get-tuple-element.23), channel_id=1, source_target_pairs={{0,2},{1,3},{2,0},{3,1},{4,6},{5,7},{6,4},{7,5},{8,10},{9,11},{10,... | collective-permute-start | bytes 786440 | tf_op jit(solution)/shard_map/ppermute | solution.py:378
  26.2 10.2 %collective-permute-start.5 = (bf16[128,1024]{1,0:T(8,128)(2,1)}, bf16[128,1024]{1,0:T(8,128)(2,1)S(1)}, u32[]{:S(2)}, u32[]{:S(2)}) collective-permute-start(bf16[128,1024]{1,0:T(8,128)(2,1)} %get-tuple-element.24), channel_id=1, source_target_pairs={{0,3},{1,2},{2,1},{3,0},{4,7},{5,6},{6,5},{7,4},{8,11},{9,10},{10,... | collective-permute-start | bytes 786440 | tf_op jit(solution)/shard_map/ppermute | solution.py:378
  32.2 9.2 %collective-permute-start.15 = (bf16[256,512]{1,0:T(8,128)(2,1)S(1)}, bf16[256,512]{1,0:T(8,128)(2,1)S(1)}, u32[]{:S(2)}, u32[]{:S(2)}) collective-permute-start(bf16[256,512]{1,0:T(8,128)(2,1)S(1)} %shard_map.70), channel_id=1, source_target_pairs={{0,4},{4,0},{8,12},{12,8},{1,5},{5,1},{9,13},{13,9},{2,6},{6,2},{1... | collective-permute-start | bytes 786440 | tf_op jit(solution)/shard_map/ppermute | solution.py:381
  36.3 10.6 %collective-permute-start.9 = (bf16[256,512]{1,0:T(8,128)(2,1)S(1)}, bf16[256,512]{1,0:T(8,128)(2,1)S(1)}, u32[]{:S(2)}, u32[]{:S(2)}) collective-permute-start(bf16[256,512]{1,0:T(8,128)(2,1)S(1)} %shard_map.63), channel_id=1, source_target_pairs={{0,4},{4,0},{8,12},{12,8},{1,5},{5,1},{9,13},{13,9},{2,6},{6,2},{1... | collective-permute-start | bytes 786440 | tf_op jit(solution)/shard_map/ppermute | solution.py:381
  43.1 9.6 %collective-permute-start.16 = (s16[528,256]{1,0:T(8,128)(2,1)S(1)}, s16[528,256]{1,0:T(8,128)(2,1)S(1)}, u32[]{:S(2)}, u32[]{:S(2)}) collective-permute-start(s16[528,256]{1,0:T(8,128)(2,1)S(1)} %shard_map.71), channel_id=1, source_target_pairs={{0,4},{4,0},{8,12},{12,8},{1,5},{5,1},{9,13},{13,9},{2,6},{6,2},{1... | collective-permute-start | bytes 811016 | tf_op jit(solution)/shard_map/ppermute | solution.py:381
  48.8 15.6 %collective-permute-start.10 = (s16[528,256]{1,0:T(8,128)(2,1)S(1)}, s16[528,256]{1,0:T(8,128)(2,1)S(1)}, u32[]{:S(2)}, u32[]{:S(2)}) collective-permute-start(s16[528,256]{1,0:T(8,128)(2,1)S(1)} %shard_map.64), channel_id=1, source_target_pairs={{0,4},{4,0},{8,12},{12,8},{1,5},{5,1},{9,13},{13,9},{2,6},{6,2},{1... | collective-permute-start | bytes 811016 | tf_op jit(solution)/shard_map/ppermute | solution.py:381
  53.0 21.1 %collective-permute-start.18 = (s16[528,256]{1,0:T(8,128)(2,1)S(1)}, s16[528,256]{1,0:T(8,128)(2,1)S(1)}, u32[]{:S(2)}, u32[]{:S(2)}) collective-permute-start(s16[528,256]{1,0:T(8,128)(2,1)S(1)} %shard_map.74), channel_id=1, source_target_pairs={{0,4},{4,0},{8,12},{12,8},{1,5},{5,1},{9,13},{13,9},{2,6},{6,2},{1... | collective-permute-start | bytes 811016 | tf_op jit(solution)/shard_map/ppermute | solution.py:381
  53.2 20.9 %collective-permute-start.17 = (s16[528,256]{1,0:T(8,128)(2,1)S(1)}, s16[528,256]{1,0:T(8,128)(2,1)S(1)}, u32[]{:S(2)}, u32[]{:S(2)}) collective-permute-start(s16[528,256]{1,0:T(8,128)(2,1)S(1)} %shard_map.72.refs_1_), channel_id=1, source_target_pairs={{0,8},{4,12},{8,0},{12,4},{1,9},{5,13},{9,1},{13,5},{2,10},{6,14},... | collective-permute-start | bytes 811016 | tf_op jit(solution)/shard_map/ppermute | solution.py:381
  64.6 2.8 %copy-start.3 = (bf16[256,512]{1,0:T(8,128)(2,1)S(1)}, bf16[256,512]{1,0:T(8,128)(2,1)}, u32[]{:S(2)}) copy-start(bf16[256,512]{1,0:T(8,128)(2,1)} %copy-done.2) | copy-start | bytes 786436
  64.6 2.8 %copy-start.6 = (bf16[128,1024]{1,0:T(8,128)(2,1)S(1)}, bf16[128,1024]{1,0:T(8,128)(2,1)}, u32[]{:S(2)}) copy-start(bf16[128,1024]{1,0:T(8,128)(2,1)} %get-tuple-element.21.refs_1_) | copy-start | bytes 786436
  64.6 2.8 %copy-start.8 = (s32[4]{0:T(128)S(1)}, s32[4]{0:T(128)}, u32[]{:S(2)}) copy-start(s32[4]{0:T(128)} %copy-done.7) | copy-start | bytes 52
  64.6 16.8 %collective-permute-start.13 = (s16[528,256]{1,0:T(8,128)(2,1)S(1)}, s16[528,256]{1,0:T(8,128)(2,1)S(1)}, u32[]{:S(2)}, u32[]{:S(2)}) collective-permute-start(s16[528,256]{1,0:T(8,128)(2,1)S(1)} %shard_map.67), channel_id=1, source_target_pairs={{0,4},{4,0},{8,12},{12,8},{1,5},{5,1},{9,13},{13,9},{2,6},{6,2},{1... | collective-permute-start | bytes 811016 | tf_op jit(solution)/shard_map/ppermute | solution.py:381
  64.7 16.7 %collective-permute-start.11 = (s16[528,256]{1,0:T(8,128)(2,1)S(1)}, s16[528,256]{1,0:T(8,128)(2,1)S(1)}, u32[]{:S(2)}, u32[]{:S(2)}) collective-permute-start(s16[528,256]{1,0:T(8,128)(2,1)S(1)} %shard_map.65.refs_1_), channel_id=1, source_target_pairs={{0,8},{4,12},{8,0},{12,4},{1,9},{5,13},{9,1},{13,5},{2,10},{6,14},... | collective-permute-start | bytes 811016 | tf_op jit(solution)/shard_map/ppermute | solution.py:381
  74.4 7.4 %collective-permute-start.19 = (bf16[128,512]{1,0:T(8,128)(2,1)S(1)}, bf16[128,512]{1,0:T(8,128)(2,1)S(1)}, u32[]{:S(2)}, u32[]{:S(2)}) collective-permute-start(bf16[128,512]{1,0:T(8,128)(2,1)S(1)} %get-tuple-element.27), channel_id=1, source_target_pairs={{0,2},{1,3},{2,0},{3,1},{4,6},{5,7},{6,4},{7,5},{8,10},{9,11},{10,... | collective-permute-start | bytes 393224 | tf_op jit(solution)/shard_map/ppermute | solution.py:378
  76.6 6.5 %collective-permute-start.20 = (bf16[128,512]{1,0:T(8,128)(2,1)S(1)}, bf16[128,512]{1,0:T(8,128)(2,1)S(1)}, u32[]{:S(2)}, u32[]{:S(2)}) collective-permute-start(bf16[128,512]{1,0:T(8,128)(2,1)S(1)} %get-tuple-element.28), channel_id=1, source_target_pairs={{0,3},{1,2},{2,1},{3,0},{4,7},{5,6},{6,5},{7,4},{8,11},{9,10},{10,... | collective-permute-start | bytes 393224 | tf_op jit(solution)/shard_map/ppermute | solution.py:378
  81.7 1.4 %collective-permute-start.14 = (bf16[128,512]{1,0:T(8,128)(2,1)S(1)}, bf16[128,512]{1,0:T(8,128)(2,1)S(1)}, u32[]{:S(2)}, u32[]{:S(2)}) collective-permute-start(bf16[128,512]{1,0:T(8,128)(2,1)S(1)} %get-tuple-element.26), channel_id=1, source_target_pairs={{0,1},{1,0},{2,3},{3,2},{4,5},{5,4},{6,7},{7,6},{8,9},{9,8},{10,11... | collective-permute-start | bytes 393224 | tf_op jit(solution)/shard_map/ppermute | solution.py:378
